TPU v7x, 512 devices: a whole 4x8x8 slice. The times are simulated.
512 devices in a mesh: gx: 16 (over z, y_hi), gy: 4 (over y_lo), gz: 8 (over x, core).
Axes of the slice: x: 4, y: 8 (y_hi: 2, y_lo: 4; y = y_hi * 4 + y_lo), z: 8, core: 2. Of those that a mesh axis runs over, the one named last changes fastest.
Arguments:
- places: float32 [4096, 3], P(('gx', 'gy', 'gz')), may hold values from 0 to 1
- scalars: float32 [4096, 256], P(('gx', 'gy', 'gz')), may hold values from -6 to 6
- vectors: float32 [4096, 3, 256], P(('gx', 'gy', 'gz')), may hold values from -6 to 6
- species: int32 [4096], P(('gx', 'gy', 'gz')), may hold values from 0 to 3
- bound_rows: int32 [4096], P(('gx', 'gy', 'gz')), may hold values from 0 to 7, as said below
- bound_count: int32 [512], P(('gx', 'gy', 'gz')), may hold values from 4 to 8, as said below
- neighbour_ids: int32 [16, 4096], P(None, ('gx', 'gy', 'gz')), may hold values from 0 to 223, as said below
- neighbour_count: int32 [4096], P(('gx', 'gy', 'gz')), may hold values from 3 to 16, as said below
- radial_first: bfloat16 [8, 64], replicated, may hold values from -2 to 2
- radial_second: bfloat16 [64, 64], replicated, may hold values from -0.75 to 0.75
- radial_third: bfloat16 [64, 1536], replicated, may hold values from -0.75 to 0.75
- energy_table: float32 [4, 256], replicated, may hold values from -6 to 6
- vector_gains: float32 [256], replicated, may hold values from -3 to 3
Outputs:
- atom_energy: float32 [4096], P(('gx', 'gy', 'gz'))
- forces: float32 [4096, 3], P(('gx', 'gy', 'gz'))
- grad_scalars: float32 [4096, 256], P(('gx', 'gy', 'gz'))
- grad_vectors: float32 [4096, 3, 256], P(('gx', 'gy', 'gz'))
Inputs may be any that keep to these rules, and one draw needn't show every extreme that they name: `bound_rows`: per domain, 8 distinct indices of its own atoms (0 to 7). `bound_count`: some domain has all 8 slots live. `neighbour_ids`: below 8: an owned atom other than the atom itself; otherwise 8 + t * 8 + b for ghost block t, never the centre block 13, and any slot b, live or not. `neighbour_count`: slots k below the count are listed neighbours. Domains differ in their largest count; some atom has 16.
All inputs are finite; a program needn't handle non-finite values.
Results may differ from a plain program's by a relative error of at most 0.014.
Values sent between devices are 32-bit elements; how exact they have to be, the bound alone decides.
A program may use at most 64 MiB of HBM per device.

v0:
```python
import jax
import jax.numpy as jnp
from jax import lax
from jax.sharding import PartitionSpec as P

SOFTENING = 0.25
SHARPNESS = 2.0
FIRST_CENTRE = 0.5
SPACING = 0.4
EDGE = 1.0


def shifted(value, axis, by):
    size = lax.axis_size(axis)
    return lax.ppermute(value, axis, [(i, (i + by) % size) for i in range(size)])


def extended(cells, sides, width):
    for axis, dim in sides:
        count = lax.axis_size(axis)
        head = lax.slice_in_dim(cells, 0, width, axis=dim)
        tail = lax.slice_in_dim(cells, cells.shape[dim] - width, cells.shape[dim], axis=dim)
        cells = jnp.concatenate(
            [
                lax.ppermute(tail, axis, [(i, (i + 1) % count) for i in range(count)]),
                cells,
                lax.ppermute(head, axis, [((i + 1) % count, i) for i in range(count)]),
            ],
            axis=dim,
        )
    return cells


def edge_messages(row_table, index_rows, usable, radial_first, radial_second, radial_third):
    slot_rows, atoms_here = index_rows.shape
    channels = (row_table.shape[1] - 3) // 4
    owned_places = row_table[:atoms_here, :3]
    far_rows = row_table[index_rows]
    separation = far_rows[:, :, :3] - owned_places[None]
    distance = jnp.sqrt(jnp.sum(separation * separation, axis=2) + SOFTENING)
    direction = separation / distance[:, :, None]
    centres = FIRST_CENTRE + SPACING * jnp.arange(radial_first.shape[0]).astype(jnp.float32)
    gauss_basis = jnp.exp(-SHARPNESS * (distance[:, :, None] - centres) ** 2)
    flat_basis = gauss_basis.reshape(slot_rows * atoms_here, -1).astype(jnp.bfloat16)
    hidden_one = jax.nn.silu(
        jnp.dot(flat_basis, radial_first, preferred_element_type=jnp.float32)
    ).astype(jnp.bfloat16)
    hidden_two = jax.nn.silu(
        jnp.dot(hidden_one, radial_second, preferred_element_type=jnp.float32)
    ).astype(jnp.bfloat16)
    path_weights = jnp.dot(hidden_two, radial_third, preferred_element_type=jnp.float32).reshape(
        slot_rows, atoms_here, 6, channels
    )
    far_scalars = far_rows[:, :, 3 : 3 + channels]
    far_vectors = far_rows[:, :, 3 + channels :].reshape(slot_rows, atoms_here, 3, channels)
    projected = jnp.sum(direction[:, :, :, None] * far_vectors, axis=2)
    crossed = jnp.stack(
        [
            far_vectors[:, :, 1] * direction[:, :, 2:3]
            - far_vectors[:, :, 2] * direction[:, :, 1:2],
            far_vectors[:, :, 2] * direction[:, :, 0:1]
            - far_vectors[:, :, 0] * direction[:, :, 2:3],
            far_vectors[:, :, 0] * direction[:, :, 1:2]
            - far_vectors[:, :, 1] * direction[:, :, 0:1],
        ],
        axis=2,
    )
    scalar_message = path_weights[:, :, 0] * far_scalars + path_weights[:, :, 1] * projected
    vector_message = (
        path_weights[:, :, 2:3] * far_scalars[:, :, None] * direction[:, :, :, None]
        + path_weights[:, :, 3:4] * far_vectors
        + path_weights[:, :, 4:5] * crossed
        + path_weights[:, :, 5:6]
        * (direction[:, :, :, None] * projected[:, :, None] - far_vectors / 3.0)
    )
    weight = usable[:, :, None]
    return (
        jnp.sum(weight * scalar_message, axis=0),
        jnp.sum(weight[:, :, :, None] * vector_message, axis=0),
    )


def atom_energy_of(scalar_out, vector_out, species_here, energy_table, vector_gains):
    channels = scalar_out.shape[1]
    onehot = (species_here[:, None] == jnp.arange(energy_table.shape[0])[None]).astype(jnp.float32)
    species_coeff = jnp.dot(onehot, energy_table, precision=lax.Precision.HIGHEST)
    squares = jnp.sum(vector_out * vector_out, axis=1)
    return (
        jnp.sum(species_coeff * jax.nn.silu(scalar_out), axis=1)
        + jnp.sum(vector_gains * squares, axis=1)
    ) * channels ** (-0.25)


def fold_gx(ghost_grid, which):

    def carry_back(ghost_slab, stride):
        return shifted(ghost_slab, "gx", stride)

    return (
        jnp.take(ghost_grid, 1, axis=which)
        + carry_back(jnp.take(ghost_grid, 0, axis=which), -1)
        + carry_back(jnp.take(ghost_grid, 2, axis=which), 1)
    )


def fold_gy(ghost_grid, which):

    def carry_back(ghost_slab, stride):
        return shifted(ghost_slab, "gy", stride)

    return (
        jnp.take(ghost_grid, 1, axis=which)
        + carry_back(jnp.take(ghost_grid, 0, axis=which), -1)
        + carry_back(jnp.take(ghost_grid, 2, axis=which), 1)
    )


def fold_gz(ghost_grid, which):

    def carry_back(ghost_slab, stride):
        return shifted(ghost_slab, "gz", stride)

    return (
        jnp.take(ghost_grid, 1, axis=which)
        + carry_back(jnp.take(ghost_grid, 0, axis=which), -1)
        + carry_back(jnp.take(ghost_grid, 2, axis=which), 1)
    )


def shards(
    places,
    scalars,
    vectors,
    species,
    bound_rows,
    bound_count,
    neighbour_ids,
    neighbour_count,
    radial_first,
    radial_second,
    radial_third,
    energy_table,
    vector_gains,
):
    atoms_here = places.shape[0]
    channels = scalars.shape[1]
    boundary = bound_rows.shape[0]
    slot_total = neighbour_ids.shape[0]
    scale = slot_total ** (-0.5)
    owned_rows = jnp.concatenate(
        [places, scalars, vectors.reshape(atoms_here, 3 * channels)], axis=1
    )
    alive_mask = (jnp.arange(boundary) < bound_count[0]).astype(jnp.float32)
    packets = (owned_rows[bound_rows] * alive_mask[:, None])[None, None, None]
    along_x = extended(packets, (("gx", 0),), 1)
    along_y = extended(along_x, (("gy", 1),), 1)
    ghosts = extended(along_y, (("gz", 2),), 1)
    unit_steps = jnp.arange(3).astype(jnp.float32) - 1.0
    displace = (
        jnp.stack(
            [
                jnp.broadcast_to(unit_steps[:, None, None], (3, 3, 3)),
                jnp.broadcast_to(unit_steps[None, :, None], (3, 3, 3)),
                jnp.broadcast_to(unit_steps[None, None, :], (3, 3, 3)),
            ],
            axis=-1,
        )
        * EDGE
    )
    ghost_places = ghosts[..., :3] + displace[:, :, :, None, :]
    ghosts = jnp.concatenate([ghost_places, ghosts[..., 3:]], axis=-1).reshape(27 * boundary, -1)
    row_table = jnp.concatenate([owned_rows, ghosts], axis=0)
    slot_width = min(slot_total, max(1, 1024 // atoms_here))
    usable_all = (jnp.arange(slot_total)[:, None] < neighbour_count[None, :]).astype(jnp.float32)
    block_count = slot_total // slot_width

    def block_sum(lookup):
        return edge_messages(
            lookup, neighbour_ids, usable_all, radial_first, radial_second, radial_third
        )

    def forward(block_index, running):
        piece_scalar, piece_vector = block_sum(row_table)
        return (running[0] + piece_scalar, running[1] + piece_vector)

    summed_scalar, summed_vector = lax.fori_loop(
        0,
        block_count,
        forward,
        (
            jnp.zeros((atoms_here, channels), jnp.float32),
            jnp.zeros((atoms_here, 3, channels), jnp.float32),
        ),
    )
    scalar_out = scalars + scale * summed_scalar
    vector_out = vectors + scale * summed_vector

    def energy_here(scalar_in, vector_in):
        return atom_energy_of(scalar_in, vector_in, species, energy_table, vector_gains)

    energies, pullback = jax.vjp(energy_here, scalar_out, vector_out)
    cotan_scalar, cotan_vector = pullback(jnp.ones_like(energies))

    def backward(block_index, grad_table):

        def block_of_table(lookup):
            return block_sum(lookup)

        unused_value, pull_block = jax.vjp(block_of_table, row_table)
        return grad_table + pull_block((scale * cotan_scalar, scale * cotan_vector))[0]

    grad_table = lax.fori_loop(0, block_count, backward, jnp.zeros_like(row_table))
    ghost_grid = grad_table[atoms_here:].reshape(3, 3, 3, boundary, -1)
    folded = fold_gz(ghost_grid, 2)
    folded = fold_gy(folded, 1)
    folded = fold_gx(folded, 0)
    returned = folded * alive_mask[:, None]
    grad_owned = grad_table[:atoms_here].at[bound_rows].add(returned)
    forces = -grad_owned[:, :3]
    grad_scalars = grad_owned[:, 3 : 3 + channels] + cotan_scalar
    grad_vectors = grad_owned[:, 3 + channels :].reshape(atoms_here, 3, channels) + cotan_vector
    return (energies, forces, grad_scalars, grad_vectors)


def solution(mesh):
    in_specs = (
        P(("gx", "gy", "gz"), None),
        P(("gx", "gy", "gz"), None),
        P(("gx", "gy", "gz"), None, None),
        P(("gx", "gy", "gz")),
        P(("gx", "gy", "gz")),
        P(("gx", "gy", "gz")),
        P(None, ("gx", "gy", "gz")),
        P(("gx", "gy", "gz")),
        P(),
        P(),
        P(),
        P(),
        P(),
    )
    out_specs = (
        P(("gx", "gy", "gz")),
        P(("gx", "gy", "gz"), None),
        P(("gx", "gy", "gz"), None),
        P(("gx", "gy", "gz"), None, None),
    )
    return jax.shard_map(shards, mesh=mesh, in_specs=in_specs, out_specs=out_specs, check_vma=False)
```

profile of v0, /device:TPU:7, one launch (start us, length us, event | category | flops | bytes accessed | tf_op | source)
XLA Modules:
  0.0 168.9 jit_solution(13940674157398385157)
XLA Ops:
  4.3 15.9 %collective-permute-start.1 = (f32[1,1,1,8,1027]{4,3,2,1,0:T(8,128)S(1)}, f32[1,1,1,8,1027]{4,3,2,1,0:T(8,128)S(1)}, u32[]{:S(2)}, u32[]{:S(2)}) collective-permute-start(f32[1,1,1,8,1027]{4,3,2,1,0:T(8,128)S(1)} %bitcast_multiply_fusion.17), channel_id=1, source_target_pairs={{32,0},{64,32},{96,64},{128,96},{160,128},{192,160},{224,192},{256... | collective-permute-start | bytes 98600 | tf_op jit(solution)/shard_map/ppermute | solution.py:27
  20.2 1.9 %collective-permute-start = (f32[1,1,1,8,1027]{4,3,2,1,0:T(8,128)S(1)}, f32[1,1,1,8,1027]{4,3,2,1,0:T(8,128)S(1)}, u32[]{:S(2)}, u32[]{:S(2)}) collective-permute-start(f32[1,1,1,8,1027]{4,3,2,1,0:T(8,128)S(1)} %bitcast_multiply_fusion.17), channel_id=1, source_target_pairs={{0,32},{32,64},{64,96},{96,128},{128,160},{160,192},{192,224},{224... | collective-permute-start | bytes 98600 | tf_op jit(solution)/shard_map/ppermute | solution.py:25
  24.7 6.3 %collective-permute-done = f32[1,1,1,8,1027]{4,3,2,1,0:T(8,128)S(1)} collective-permute-done((f32[1,1,1,8,1027]{4,3,2,1,0:T(8,128)S(1)}, f32[1,1,1,8,1027]{4,3,2,1,0:T(8,128)S(1)}, u32[]{:S(2)}, u32[]{:S(2)}) %collective-permute-start) | collective-permute-done | bytes 32896 | tf_op jit(solution)/shard_map/ppermute | solution.py:25
  31.0 2.5 %collective-permute-start.3 = (f32[3,1,1,8,1027]{4,3,2,1,0:T(8,128)S(1)}, f32[3,1,1,8,1027]{4,3,2,1,0:T(8,128)S(1)}, u32[]{:S(2)}, u32[]{:S(2)}) collective-permute-start(f32[3,1,1,8,1027]{4,3,2,1,0:T(8,128)S(1)} %pad_maximum_fusion.3), channel_id=1, source_target_pairs={{8,0},{16,8},{24,16},{0,24},{9,1},{17,9},{25,17},{1,25},{10,2},{18... | collective-permute-start | bytes 295784 | tf_op jit(solution)/shard_map/ppermute | solution.py:27
  33.6 2.8 %collective-permute-start.2 = (f32[3,1,1,8,1027]{4,3,2,1,0:T(8,128)S(1)}, f32[3,1,1,8,1027]{4,3,2,1,0:T(8,128)S(1)}, u32[]{:S(2)}, u32[]{:S(2)}) collective-permute-start(f32[3,1,1,8,1027]{4,3,2,1,0:T(8,128)S(1)} %pad_maximum_fusion.3), channel_id=1, source_target_pairs={{0,8},{8,16},{16,24},{24,0},{1,9},{9,17},{17,25},{25,1},{2,10},{10... | collective-permute-start | bytes 295784 | tf_op jit(solution)/shard_map/ppermute | solution.py:25
  36.5 4.3 %collective-permute-done.2 = f32[3,1,1,8,1027]{4,3,2,1,0:T(8,128)S(1)} collective-permute-done((f32[3,1,1,8,1027]{4,3,2,1,0:T(8,128)S(1)}, f32[3,1,1,8,1027]{4,3,2,1,0:T(8,128)S(1)}, u32[]{:S(2)}, u32[]{:S(2)}) %collective-permute-start.2) | collective-permute-done | bytes 98624 | tf_op jit(solution)/shard_map/ppermute | solution.py:25
  40.9 3.5 %collective-permute-start.5 = (f32[3,3,1,8,1027]{4,3,2,1,0:T(8,128)S(1)}, f32[3,3,1,8,1027]{4,3,2,1,0:T(8,128)S(1)}, u32[]{:S(2)}, u32[]{:S(2)}) collective-permute-start(f32[3,3,1,8,1027]{4,3,2,1,0:T(8,128)S(1)} %pad_maximum_fusion.2), channel_id=1, source_target_pairs={{1,0},{2,1},{3,2},{4,3},{5,4},{6,5},{7,6},{0,7},{9,8},{10,9},{11,1... | collective-permute-start | bytes 887336 | tf_op jit(solution)/shard_map/ppermute | solution.py:27
  44.6 1.3 broadcast_multiply_fusion.5
  45.8 3.5 %collective-permute-done.5 = f32[3,3,1,8,1027]{4,3,2,1,0:T(8,128)S(1)} collective-permute-done((f32[3,3,1,8,1027]{4,3,2,1,0:T(8,128)S(1)}, f32[3,3,1,8,1027]{4,3,2,1,0:T(8,128)S(1)}, u32[]{:S(2)}, u32[]{:S(2)}) %collective-permute-start.5) | collective-permute-done | bytes 295808 | tf_op jit(solution)/shard_map/ppermute | solution.py:27
  55.9 1.3 copy.517
  57.2 1.3 copy.462
  59.7 2.2 %copy.466 = f32[16,8,256]{2,1,0:T(8,128)} copy(f32[16,8,256]{0,1,2:T(8,128)} %fusion.10) | data formatting | bytes 262144 | tf_op jit(solution)/shard_map/while/body/eval_jaxpr/mul | solution.py:70
  64.1 1.2 multiply_reduce_fusion.2
  68.8 1.4 copy.522
  70.1 2.2 %copy.523 = f32[16,8,1,256]{0,1,3,2:T(8,128)} copy(f32[16,8,1,256]{3,1,2,0:T(8,128)} %get-tuple-element.240) | data formatting | bytes 262144
  72.3 2.2 %fusion.13 = f32[8,256]{0,1:T(8,128)S(1)} fusion(f32[16,8,256]{0,1,2:T(8,128)} %copy.462, f32[16,8,1,256]{0,1,3,2:T(8,128)} %copy.523, f32[16,8,256]{0,1,2:T(8,128)S(1)} %copy.518, f32[16,8,1,256]{0,1,3,2:T(8,128)} %copy.522, f32[16,8]{0,1:T(8,128)S(1)} %fusion.98), kind=kLoop, calls=%fused_computation.29 | loop fusion | flops 161792 | bytes 532992 | tf_op jit(solution)/shard_map/while/body/eval_jaxpr/reduce_sum | solution.py:78
  74.6 1.4 broadcast_multiply_fusion.4
  76.2 2.6 %bitcast_multiply_fusion.1 = f32[16,8,1,256]{0,1,3,2:T(8,128)} fusion(f32[16,8,256]{0,1,2:T(8,128)} %copy.462, f32[8,256]{0,1:T(8,128)S(1)} %copy.493, f32[16,8]{0,1:T(8,128)S(1)} %fusion.98), kind=kLoop, calls=%fused_computation.23 | loop fusion | flops 65536 | bytes 270848 | tf_op jit(solution)/shard_map/while/body/eval_jaxpr/transpose(jvp())/mul | solution.py:68
  78.9 1.4 copy.485
  80.2 1.4 copy.486
  81.6 1.4 copy.488
  82.9 1.4 copy.489
  84.3 1.4 copy.491
  85.6 1.4 copy.492
  87.0 2.2 %copy.500 = f32[16,8,256]{0,1,2:T(8,128)} copy(f32[16,8,256]{2,1,0:T(8,128)} %get-tuple-element.255) | data formatting | bytes 262144 | tf_op jit(solution)/shard_map/while/body/eval_jaxpr/transpose(jvp())/reduce_sum | solution.py:72
  89.2 2.2 %copy.494 = f32[16,8,256]{0,1,2:T(8,128)} copy(f32[16,8,256]{2,1,0:T(8,128)} %get-tuple-element.264) | data formatting | bytes 262144 | tf_op jit(solution)/shard_map/while/body/eval_jaxpr/transpose(jvp())/reduce_sum | solution.py:74
  91.4 2.9 %fusion.7 = f32[16,8,256]{0,1,2:T(8,128)} fusion(f32[16,8,256]{0,1,2:T(8,128)} %copy.494, f32[16,8,1,256]{0,1,3,2:T(8,128)} %copy.523, f32[8,256]{0,1:T(8,128)S(1)} %copy.493, f32[16,8]{0,1:T(8,128)S(1)} %fusion.98), kind=kLoop, calls=%fused_computation.19 | loop fusion | flops 98304 | bytes 401920 | tf_op jit(solution)/shard_map/while/body/eval_jaxpr/transpose(jvp())/add_any | solution.py:68
  94.3 2.2 %copy.495 = f32[16,8,256]{2,1,0:T(8,128)} copy(f32[16,8,256]{0,1,2:T(8,128)} %fusion.7) | data formatting | bytes 262144 | tf_op jit(solution)/shard_map/while/body/eval_jaxpr/transpose(jvp())/add_any | solution.py:68
  96.5 3.2 %fusion.41 = (f32[16,8,256]{2,1,0:T(8,128)}, f32[16,8,256]{2,1,0:T(8,128)}, f32[16,8,3]{1,2,0:T(4,128)}, f32[16,8,3]{1,2,0:T(4,128)}, f32[16,8,256]{2,1,0:T(8,12...) fusion(f32[16,8,3,256]{3,1,2,0:T(8,128)S(1)} %bitcast.213, f32[8,3,256]{2,0,1:T(8,128)S(1)} %fusion.85, ...), kind=kLoop, calls=%fused_computation.69 | loop fusion | flops 2751360 | bytes 2652672 | tf_op jit(solution)/shard_map/while/body/eval_jaxpr/transpose(jvp())/reduce_sum | solution.py:73
  102.2 2.2 %copy.497 = f32[16,8,256]{0,1,2:T(8,128)} copy(f32[16,8,256]{2,1,0:T(8,128)} %get-tuple-element.217) | data formatting | bytes 262144 | tf_op jit(solution)/shard_map/while/body/eval_jaxpr/transpose(jvp())/reduce_sum | solution.py:73
  104.5 2.2 %copy.501 = f32[16,8,256]{0,1,2:T(8,128)} copy(f32[16,8,256]{2,1,0:T(8,128)} %get-tuple-element.218) | data formatting | bytes 262144 | tf_op jit(solution)/shard_map/while/body/eval_jaxpr/transpose(jvp())/reduce_sum | solution.py:71
  106.7 2.3 %copy.502 = f32[16,8,256]{0,1,2:T(8,128)} copy(f32[16,8,256]{2,1,0:T(8,128)} %get-tuple-element.221) | data formatting | bytes 262144 | tf_op jit(solution)/shard_map/while/body/eval_jaxpr/transpose(jvp())/reduce_sum | solution.py:70
  109.0 3.1 %fusion.9 = (f32[16,8,256]{0,1,2:T(8,128)}, f32[16,8,1,256]{0,1,3,2:T(8,128)S(1)}, f32[16,8,1,256]{0,1,3,2:T(8,128)S(1)}) fusion(f32[16,8,1,256]{0,1,3,2:T(8,128)S(1)} %copy.517, f32[16,8,256]{0,1,2:T(8,128)} %copy.502, f32[16,8,1,256]{0,1,3,2:T(8,128)} %copy.522, f32[8,256]{0,1:T(8,128)S(1)} %copy.493, f32[16,8]{0,1:T(8,128)S(1)} %fusion.98, ...), kind=kLoop, calls=%fused_computation.21 | loop fusion | flops 196608 | bytes 926208 | tf_op jit(solution)/shard_map/while/body/eval_jaxpr/transpose(jvp())/add_any | solution.py:68
  113.0 2.7 %copy.505 = bf16[16,8,6,256]{3,1,2,0:T(8,128)(2,1)} copy(bf16[16,8,6,256]{0,1,3,2:T(8,128)(2,1)S(1)} %pad_add_fusion) | data formatting | bytes 786432 | tf_op jit(solution)/shard_map/while/body/eval_jaxpr/transpose(jvp())/add_any | solution.py:68
  115.8 1.2 fusion.1
  118.7 2.1 %copy.508 = f32[16,8,768]{0,1,2:T(8,128)S(1)} copy(f32[16,8,768]{2,1,0:T(8,128)} %bitcast.230) | data formatting | bytes 786432 | tf_op jit(solution)/shard_map/while/body/eval_jaxpr/transpose(jvp())/reshape | solution.py:55
  120.8 4.4 %pad_add_fusion.1 = f32[16,8,1027]{0,1,2:T(8,128)} fusion(f32[16,8,3]{0,1,2:T(8,128)S(1)} %get-tuple-element.224, f32[16,8,256]{0,1,2:T(8,128)} %get-tuple-element.229, f32[16,8,768]{0,1,2:T(8,128)S(1)} %copy.508), kind=kLoop, calls=%fused_computation.5 | loop fusion | flops 262912 | bytes 1051648 | tf_op jit(solution)/shard_map/while/body/eval_jaxpr/transpose(jvp())/add_any | solution.py:39
  125.2 3.3 %copy.510 = f32[16,8,1027]{2,1,0:T(8,128)S(1)} copy(f32[16,8,1027]{0,1,2:T(8,128)} %pad_add_fusion.1) | data formatting | bytes 1051648 | tf_op jit(solution)/shard_map/while/body/eval_jaxpr/transpose(jvp())/add_any | solution.py:39
  128.6 2.3 %scatter_custom_fusion = f32[224,1027]{1,0:T(8,128)S(1)} fusion(f32[224,1027]{1,0:T(8,128)S(1)} %pad.100, s32[128]{0:T(128)} %copy-done.54, f32[16,8,1027]{2,1,0:T(8,128)S(1)} %copy.510), kind=kCustom, calls=%fused_computation.55 | custom fusion | flops 131456 | bytes 1510016 | tf_op jit(solution)/shard_map/while/body/eval_jaxpr/transpose(jvp())/scatter-add | solution.py:38
  131.1 3.0 %collective-permute-start.7 = (f32[3,3,8,1027]{3,2,0,1:T(8,128)S(1)}, f32[3,3,8,1027]{3,2,0,1:T(8,128)S(1)}, u32[]{:S(2)}, u32[]{:S(2)}) collective-permute-start(f32[3,3,8,1027]{3,2,0,1:T(8,128)S(1)} %bitcast.232), channel_id=1, source_target_pairs={{0,1},{1,2},{2,3},{3,4},{4,5},{5,6},{6,7},{7,0},{8,9},{9,10},{10,1... | collective-permute-start | bytes 887336 | tf_op jit(solution)/shard_map/ppermute | solution.py:15
  134.1 4.1 %collective-permute-done.7 = f32[3,3,8,1027]{3,2,0,1:T(8,128)S(1)} collective-permute-done((f32[3,3,8,1027]{3,2,0,1:T(8,128)S(1)}, f32[3,3,8,1027]{3,2,0,1:T(8,128)S(1)}, u32[]{:S(2)}, u32[]{:S(2)}) %collective-permute-start.7) | collective-permute-done | bytes 295808 | tf_op jit(solution)/shard_map/ppermute | solution.py:15
  138.2 3.7 %collective-permute-done.6 = f32[3,3,8,1027]{3,2,0,1:T(8,128)S(1)} collective-permute-done((f32[3,3,8,1027]{3,2,0,1:T(8,128)S(1)}, f32[3,3,8,1027]{3,2,0,1:T(8,128)S(1)}, u32[]{:S(2)}, u32[]{:S(2)}) %collective-permute-start.6) | collective-permute-done | bytes 295808 | tf_op jit(solution)/shard_map/ppermute | solution.py:15
  142.0 1.9 %collective-permute-start.8 = (f32[3,8,1027]{2,1,0:T(8,128)S(1)}, f32[3,8,1027]{2,1,0:T(8,128)S(1)}, u32[]{:S(2)}, u32[]{:S(2)}) collective-permute-start(f32[3,8,1027]{2,1,0:T(8,128)S(1)} %get-tuple-element.256), channel_id=1, source_target_pairs={{0,24},{8,0},{16,8},{24,16},{1,25},{9,1},{17,9},{25,17},{2,26},{10... | collective-permute-start | bytes 295784 | tf_op jit(solution)/shard_map/ppermute | solution.py:15
  143.9 3.4 %collective-permute-start.9 = (f32[3,8,1027]{2,1,0:T(8,128)S(1)}, f32[3,8,1027]{2,1,0:T(8,128)S(1)}, u32[]{:S(2)}, u32[]{:S(2)}) collective-permute-start(f32[3,8,1027]{2,1,0:T(8,128)S(1)} %get-tuple-element.257), channel_id=1, source_target_pairs={{0,8},{8,16},{16,24},{24,0},{1,9},{9,17},{17,25},{25,1},{2,10},{10... | collective-permute-start | bytes 295784 | tf_op jit(solution)/shard_map/ppermute | solution.py:15
  147.5 3.7 %collective-permute-done.9 = f32[3,8,1027]{2,1,0:T(8,128)S(1)} collective-permute-done((f32[3,8,1027]{2,1,0:T(8,128)S(1)}, f32[3,8,1027]{2,1,0:T(8,128)S(1)}, u32[]{:S(2)}, u32[]{:S(2)}) %collective-permute-start.9) | collective-permute-done | bytes 98624 | tf_op jit(solution)/shard_map/ppermute | solution.py:15
  151.2 3.4 %collective-permute-start.10 = (f32[8,1027]{1,0:T(8,128)S(1)}, f32[8,1027]{1,0:T(8,128)S(1)}, u32[]{:S(2)}, u32[]{:S(2)}) collective-permute-start(f32[8,1027]{1,0:T(8,128)S(1)} %get-tuple-element.259), channel_id=1, source_target_pairs={{0,480},{32,0},{64,32},{96,64},{128,96},{160,128},{192,160},{224,1... | collective-permute-start | bytes 98600 | tf_op jit(solution)/shard_map/ppermute | solution.py:15
  154.7 5.7 %collective-permute-start.11 = (f32[8,1027]{1,0:T(8,128)S(1)}, f32[8,1027]{1,0:T(8,128)S(1)}, u32[]{:S(2)}, u32[]{:S(2)}) collective-permute-start(f32[8,1027]{1,0:T(8,128)S(1)} %get-tuple-element.260), channel_id=1, source_target_pairs={{0,32},{32,64},{64,96},{96,128},{128,160},{160,192},{192,224},{224... | collective-permute-start | bytes 98600 | tf_op jit(solution)/shard_map/ppermute | solution.py:15
  160.5 4.9 %collective-permute-done.11 = f32[8,1027]{1,0:T(8,128)S(1)} collective-permute-done((f32[8,1027]{1,0:T(8,128)S(1)}, f32[8,1027]{1,0:T(8,128)S(1)}, u32[]{:S(2)}, u32[]{:S(2)}) %collective-permute-start.11) | collective-permute-done | bytes 32896 | tf_op jit(solution)/shard_map/ppermute | solution.py:15
  (233 shorter events, 28.0 us)
Async XLA Ops:
  0.6 51.9 %copy-start = (bf16[64,1536]{1,0:T(8,128)(2,1)S(1)}, bf16[64,1536]{1,0:T(8,128)(2,1)}, u32[]{:S(2)}) copy-start(bf16[64,1536]{1,0:T(8,128)(2,1)} %param.41) | copy-start | bytes 589828
  4.3 20.4 %collective-permute-start.1 = (f32[1,1,1,8,1027]{4,3,2,1,0:T(8,128)S(1)}, f32[1,1,1,8,1027]{4,3,2,1,0:T(8,128)S(1)}, u32[]{:S(2)}, u32[]{:S(2)}) collective-permute-start(f32[1,1,1,8,1027]{4,3,2,1,0:T(8,128)S(1)} %bitcast_multiply_fusion.17), channel_id=1, source_target_pairs={{32,0},{64,32},{96,64},{128,96},{160,128},{192,160},{224,192},{256... | collective-permute-start | bytes 98600 | tf_op jit(solution)/shard_map/ppermute | solution.py:27
  20.2 10.8 %collective-permute-start = (f32[1,1,1,8,1027]{4,3,2,1,0:T(8,128)S(1)}, f32[1,1,1,8,1027]{4,3,2,1,0:T(8,128)S(1)}, u32[]{:S(2)}, u32[]{:S(2)}) collective-permute-start(f32[1,1,1,8,1027]{4,3,2,1,0:T(8,128)S(1)} %bitcast_multiply_fusion.17), channel_id=1, source_target_pairs={{0,32},{32,64},{64,96},{96,128},{128,160},{160,192},{192,224},{224... | collective-permute-start | bytes 98600 | tf_op jit(solution)/shard_map/ppermute | solution.py:25
  24.0 12.5 %copy-start.54 = (s32[128]{0:T(128)}, s32[128]{0:T(128)S(1)}, u32[]{:S(2)}) copy-start(s32[128]{0:T(128)S(1)} %reshape.511) | copy-start | bytes 1540
  31.0 5.5 %collective-permute-start.3 = (f32[3,1,1,8,1027]{4,3,2,1,0:T(8,128)S(1)}, f32[3,1,1,8,1027]{4,3,2,1,0:T(8,128)S(1)}, u32[]{:S(2)}, u32[]{:S(2)}) collective-permute-start(f32[3,1,1,8,1027]{4,3,2,1,0:T(8,128)S(1)} %pad_maximum_fusion.3), channel_id=1, source_target_pairs={{8,0},{16,8},{24,16},{0,24},{9,1},{17,9},{25,17},{1,25},{10,2},{18... | collective-permute-start | bytes 295784 | tf_op jit(solution)/shard_map/ppermute | solution.py:27
  33.6 7.3 %collective-permute-start.2 = (f32[3,1,1,8,1027]{4,3,2,1,0:T(8,128)S(1)}, f32[3,1,1,8,1027]{4,3,2,1,0:T(8,128)S(1)}, u32[]{:S(2)}, u32[]{:S(2)}) collective-permute-start(f32[3,1,1,8,1027]{4,3,2,1,0:T(8,128)S(1)} %pad_maximum_fusion.3), channel_id=1, source_target_pairs={{0,8},{8,16},{16,24},{24,0},{1,9},{9,17},{17,25},{25,1},{2,10},{10... | collective-permute-start | bytes 295784 | tf_op jit(solution)/shard_map/ppermute | solution.py:25
  40.9 8.4 %collective-permute-start.5 = (f32[3,3,1,8,1027]{4,3,2,1,0:T(8,128)S(1)}, f32[3,3,1,8,1027]{4,3,2,1,0:T(8,128)S(1)}, u32[]{:S(2)}, u32[]{:S(2)}) collective-permute-start(f32[3,3,1,8,1027]{4,3,2,1,0:T(8,128)S(1)} %pad_maximum_fusion.2), channel_id=1, source_target_pairs={{1,0},{2,1},{3,2},{4,3},{5,4},{6,5},{7,6},{0,7},{9,8},{10,9},{11,1... | collective-permute-start | bytes 887336 | tf_op jit(solution)/shard_map/ppermute | solution.py:27
  44.5 4.9 %collective-permute-start.4 = (f32[3,3,1,8,1027]{4,3,2,1,0:T(8,128)S(1)}, f32[3,3,1,8,1027]{4,3,2,1,0:T(8,128)S(1)}, u32[]{:S(2)}, u32[]{:S(2)}) collective-permute-start(f32[3,3,1,8,1027]{4,3,2,1,0:T(8,128)S(1)} %pad_maximum_fusion.2), channel_id=1, source_target_pairs={{0,1},{1,2},{2,3},{3,4},{4,5},{5,6},{6,7},{7,0},{8,9},{9,10},{10,1... | collective-permute-start | bytes 887336 | tf_op jit(solution)/shard_map/ppermute | solution.py:25
  44.6 7.6 %copy-start.65 = (f32[8]{0:T(128)}, f32[8]{0:T(128)S(1)}, u32[]{:S(2)}) copy-start(f32[8]{0:T(128)S(1)} %multiply_add_fusion.1) | copy-start | bytes 100
  61.9 5.8 %copy-start.27 = (f32[16,8]{1,0:T(8,128)S(1)}, f32[16,8]{1,0:T(8,128)}, u32[]{:S(2)}) copy-start(f32[16,8]{1,0:T(8,128)} %copy-done.26) | copy-start | bytes 1540
  61.9 5.8 %copy-start.29 = (f32[16,8]{1,0:T(8,128)S(1)}, f32[16,8]{1,0:T(8,128)}, u32[]{:S(2)}) copy-start(f32[16,8]{1,0:T(8,128)} %copy-done.28) | copy-start | bytes 1540
  62.0 5.8 %copy-start.31 = (f32[16,8]{1,0:T(8,128)S(1)}, f32[16,8]{1,0:T(8,128)}, u32[]{:S(2)}) copy-start(f32[16,8]{1,0:T(8,128)} %copy-done.30) | copy-start | bytes 1540
  65.3 9.2 %copy-start.20 = (f32[8,768]{1,0:T(8,128)}, f32[8,768]{1,0:T(8,128)S(1)}, u32[]{:S(2)}) copy-start(f32[8,768]{1,0:T(8,128)S(1)} %broadcast_multiply_fusion.3) | copy-start | bytes 73732
  67.7 6.9 %copy-start.49 = (f32[8,256]{1,0:T(8,128)S(1)}, f32[8,256]{1,0:T(8,128)}, u32[]{:S(2)}) copy-start(f32[8,256]{1,0:T(8,128)} %param.32) | copy-start | bytes 24580
  67.7 6.9 %copy-start.60 = (f32[4,256]{1,0:T(4,128)S(1)}, f32[4,256]{1,0:T(4,128)}, u32[]{:S(2)}) copy-start(f32[4,256]{1,0:T(4,128)} %param.42) | copy-start | bytes 12292
  67.7 6.9 %copy-start.63 = (s32[8]{0:T(128)S(1)}, s32[8]{0:T(128)}, u32[]{:S(2)}) copy-start(s32[8]{0:T(128)} %param.34) | copy-start | bytes 100
  76.2 20.3 %copy-start.5 = (f32[16,8,256]{2,1,0:T(8,128)S(1)}, f32[16,8,256]{2,1,0:T(8,128)}, u32[]{:S(2)}) copy-start(f32[16,8,256]{2,1,0:T(8,128)} %copy.466) | copy-start | bytes 393220
  76.2 20.3 %copy-start.6 = (f32[16,8,256]{2,1,0:T(8,128)S(1)}, f32[16,8,256]{2,1,0:T(8,128)}, u32[]{:S(2)}) copy-start(f32[16,8,256]{2,1,0:T(8,128)} %get-tuple-element.235) | copy-start | bytes 393220
  76.2 20.3 %copy-start.17 = (f32[16,8,3]{1,2,0:T(4,128)S(1)}, f32[16,8,3]{1,2,0:T(4,128)}, u32[]{:S(2)}) copy-start(f32[16,8,3]{1,2,0:T(4,128)} %copy-done.15) | copy-start | bytes 4612
  76.2 20.3 %copy-start.19 = (f32[16,8,1,256]{3,1,2,0:T(8,128)S(1)}, f32[16,8,1,256]{3,1,2,0:T(8,128)}, u32[]{:S(2)}) copy-start(f32[16,8,1,256]{3,1,2,0:T(8,128)} %get-tuple-element.241) | copy-start | bytes 393220
  76.2 20.3 %copy-start.25 = (f32[16,8]{1,0:T(8,128)S(1)}, f32[16,8]{1,0:T(8,128)}, u32[]{:S(2)}) copy-start(f32[16,8]{1,0:T(8,128)} %copy.464) | copy-start | bytes 1540
  112.1 4.9 %copy-start.39 = (f32[128,64]{0,1:T(8,128)S(1)}, f32[128,64]{0,1:T(8,128)}, u32[]{:S(2)}) copy-start(f32[128,64]{0,1:T(8,128)} %copy-done.38) | copy-start | bytes 98308
  112.1 4.9 %copy-start.57 = (f32[128]{0:T(128)S(1)}, f32[128]{0:T(128)}, u32[]{:S(2)}) copy-start(f32[128]{0:T(128)} %copy-done.56) | copy-start | bytes 1540
  112.1 4.9 %copy-start.59 = (bf16[64,64]{1,0:T(8,128)(2,1)S(1)}, bf16[64,64]{1,0:T(8,128)(2,1)}, u32[]{:S(2)}) copy-start(bf16[64,64]{1,0:T(8,128)(2,1)} %param.40) | copy-start | bytes 24580
  112.1 4.9 %copy-start.62 = (bf16[8,64]{1,0:T(8,128)(2,1)S(1)}, bf16[8,64]{1,0:T(8,128)(2,1)}, u32[]{:S(2)}) copy-start(bf16[8,64]{1,0:T(8,128)(2,1)} %param.39) | copy-start | bytes 3076
  112.9 5.3 %copy-start.35 = (f32[8,3]{0,1:T(4,128)S(1)}, f32[8,3]{0,1:T(4,128)}, u32[]{:S(2)}) copy-start(f32[8,3]{0,1:T(4,128)} %param.31) | copy-start | bytes 292
  112.9 5.3 %copy-start.40 = (f32[16,8]{0,1:T(8,128)S(1)}, f32[16,8]{0,1:T(8,128)}, u32[]{:S(2)}) copy-start(f32[16,8]{0,1:T(8,128)} %get-tuple-element.271) | copy-start | bytes 1540
  112.9 5.3 %copy-start.41 = (f32[16,8]{0,1:T(8,128)S(1)}, f32[16,8]{0,1:T(8,128)}, u32[]{:S(2)}) copy-start(f32[16,8]{0,1:T(8,128)} %copy.485) | copy-start | bytes 1540
  113.0 5.3 %copy-start.42 = (f32[16,8]{0,1:T(8,128)S(1)}, f32[16,8]{0,1:T(8,128)}, u32[]{:S(2)}) copy-start(f32[16,8]{0,1:T(8,128)} %copy.486) | copy-start | bytes 1540
  113.0 5.3 %copy-start.43 = (f32[16,8]{0,1:T(8,128)S(1)}, f32[16,8]{0,1:T(8,128)}, u32[]{:S(2)}) copy-start(f32[16,8]{0,1:T(8,128)} %copy.488) | copy-start | bytes 1540
  113.0 5.3 %copy-start.44 = (f32[16,8]{0,1:T(8,128)S(1)}, f32[16,8]{0,1:T(8,128)}, u32[]{:S(2)}) copy-start(f32[16,8]{0,1:T(8,128)} %copy.489) | copy-start | bytes 1540
  113.0 5.3 %copy-start.45 = (f32[16,8]{0,1:T(8,128)S(1)}, f32[16,8]{0,1:T(8,128)}, u32[]{:S(2)}) copy-start(f32[16,8]{0,1:T(8,128)} %copy.491) | copy-start | bytes 1540
  113.0 5.3 %copy-start.46 = (f32[16,8]{0,1:T(8,128)S(1)}, f32[16,8]{0,1:T(8,128)}, u32[]{:S(2)}) copy-start(f32[16,8]{0,1:T(8,128)} %copy.492) | copy-start | bytes 1540
  113.0 5.4 %copy-start.37 = (f32[16,8]{0,1:T(8,128)S(1)}, f32[16,8]{0,1:T(8,128)}, u32[]{:S(2)}) copy-start(f32[16,8]{0,1:T(8,128)} %copy-done.36) | copy-start | bytes 1540
  113.0 5.4 %copy-start.33 = (f32[16,8]{0,1:T(8,128)S(1)}, f32[16,8]{0,1:T(8,128)}, u32[]{:S(2)}) copy-start(f32[16,8]{0,1:T(8,128)} %copy-done.32) | copy-start | bytes 1540
  130.9 34.6 %copy-start.53 = (f32[8]{0:T(128)S(1)}, f32[8]{0:T(128)}, u32[]{:S(2)}) copy-start(f32[8]{0:T(128)} %copy-done.52) | copy-start | bytes 100
  130.9 35.5 %copy-start.50 = (f32[8,256]{1,0:T(8,128)S(1)}, f32[8,256]{1,0:T(8,128)}, u32[]{:S(2)}) copy-start(f32[8,256]{1,0:T(8,128)} %get-tuple-element.228) | copy-start | bytes 24580
  130.9 36.8 %copy-start.21 = (f32[8,768]{1,0:T(8,128)S(1)}, f32[8,768]{1,0:T(8,128)}, u32[]{:S(2)}) copy-start(f32[8,768]{1,0:T(8,128)} %copy-done.20) | copy-start | bytes 73732
  130.9 36.8 %copy-start.23 = (f32[8,3,256]{2,0,1:T(8,128)S(1)}, f32[8,3,256]{2,0,1:T(8,128)}, u32[]{:S(2)}) copy-start(f32[8,3,256]{2,0,1:T(8,128)} %param.33) | copy-start | bytes 73732
  130.9 36.8 %copy-start.48 = (f32[256]{0:T(256)S(1)}, f32[256]{0:T(256)}, u32[]{:S(2)}) copy-start(f32[256]{0:T(256)} %broadcast_multiply_fusion.5) | copy-start | bytes 3076
  130.9 37.4 %copy-start.51 = (f32[256]{0:T(256)S(1)}, f32[256]{0:T(256)}, u32[]{:S(2)}) copy-start(f32[256]{0:T(256)} %param.43) | copy-start | bytes 3076
  130.9 37.5 %copy-start.64 = (f32[8]{0:T(128)S(1)}, f32[8]{0:T(128)}, u32[]{:S(2)}) copy-start(f32[8]{0:T(128)} %get-tuple-element.267) | copy-start | bytes 100
  131.1 7.0 %collective-permute-start.7 = (f32[3,3,8,1027]{3,2,0,1:T(8,128)S(1)}, f32[3,3,8,1027]{3,2,0,1:T(8,128)S(1)}, u32[]{:S(2)}, u32[]{:S(2)}) collective-permute-start(f32[3,3,8,1027]{3,2,0,1:T(8,128)S(1)} %bitcast.232), channel_id=1, source_target_pairs={{0,1},{1,2},{2,3},{3,4},{4,5},{5,6},{6,7},{7,0},{8,9},{9,10},{10,1... | collective-permute-start | bytes 887336 | tf_op jit(solution)/shard_map/ppermute | solution.py:15
  134.1 7.8 %collective-permute-start.6 = (f32[3,3,8,1027]{3,2,0,1:T(8,128)S(1)}, f32[3,3,8,1027]{3,2,0,1:T(8,128)S(1)}, u32[]{:S(2)}, u32[]{:S(2)}) collective-permute-start(f32[3,3,8,1027]{3,2,0,1:T(8,128)S(1)} %bitcast.231), channel_id=1, source_target_pairs={{0,7},{1,0},{2,1},{3,2},{4,3},{5,4},{6,5},{7,6},{8,15},{9,8},{10,9... | collective-permute-start | bytes 887336 | tf_op jit(solution)/shard_map/ppermute | solution.py:15
  142.0 5.5 %collective-permute-start.8 = (f32[3,8,1027]{2,1,0:T(8,128)S(1)}, f32[3,8,1027]{2,1,0:T(8,128)S(1)}, u32[]{:S(2)}, u32[]{:S(2)}) collective-permute-start(f32[3,8,1027]{2,1,0:T(8,128)S(1)} %get-tuple-element.256), channel_id=1, source_target_pairs={{0,24},{8,0},{16,8},{24,16},{1,25},{9,1},{17,9},{25,17},{2,26},{10... | collective-permute-start | bytes 295784 | tf_op jit(solution)/shard_map/ppermute | solution.py:15
  143.9 7.3 %collective-permute-start.9 = (f32[3,8,1027]{2,1,0:T(8,128)S(1)}, f32[3,8,1027]{2,1,0:T(8,128)S(1)}, u32[]{:S(2)}, u32[]{:S(2)}) collective-permute-start(f32[3,8,1027]{2,1,0:T(8,128)S(1)} %get-tuple-element.257), channel_id=1, source_target_pairs={{0,8},{8,16},{16,24},{24,0},{1,9},{9,17},{17,25},{25,1},{2,10},{10... | collective-permute-start | bytes 295784 | tf_op jit(solution)/shard_map/ppermute | solution.py:15
  151.2 9.2 %collective-permute-start.10 = (f32[8,1027]{1,0:T(8,128)S(1)}, f32[8,1027]{1,0:T(8,128)S(1)}, u32[]{:S(2)}, u32[]{:S(2)}) collective-permute-start(f32[8,1027]{1,0:T(8,128)S(1)} %get-tuple-element.259), channel_id=1, source_target_pairs={{0,480},{32,0},{64,32},{96,64},{128,96},{160,128},{192,160},{224,1... | collective-permute-start | bytes 98600 | tf_op jit(solution)/shard_map/ppermute | solution.py:15
  154.7 10.7 %collective-permute-start.11 = (f32[8,1027]{1,0:T(8,128)S(1)}, f32[8,1027]{1,0:T(8,128)S(1)}, u32[]{:S(2)}, u32[]{:S(2)}) collective-permute-start(f32[8,1027]{1,0:T(8,128)S(1)} %get-tuple-element.260), channel_id=1, source_target_pairs={{0,32},{32,64},{64,96},{96,128},{128,160},{160,192},{192,224},{224... | collective-permute-start | bytes 98600 | tf_op jit(solution)/shard_map/ppermute | solution.py:15
  (32 other events, 82.1 us)
where the time goes:
time: 170 us; the launch traced here: 169 us
  local copies, waits for them, and re-layouts  50.9 us (30%)
  starting transfers between devices  44.2 us (26%)
  other arithmetic  36.1 us (21%)
  waiting for transfers between devices  31 us (18%)
  matrix products  4.38 us (3%)
  between operations  2.4 us (1%)
    ppermute x3, starting transfers between devices, extended(): lax.ppermute(head, axis, [((i + 1) % count, i) for i in range(count)])  22 us
    ppermute x6, starting transfers between devices, shifted(): lax.ppermute(value, axis, [(i, (i + by) % size) for i in range(size)])  17.5 us
    ppermute x6, waiting for transfers between devices, shifted(): lax.ppermute(value, axis, [(i, (i + by) % size) for i in range(size)])  16.6 us
    ppermute x3, waiting for transfers between devices, extended(): lax.ppermute(tail, axis, [(i, (i + 1) % count) for i in range(count)])  10.7 us
    unnamed x145, local copies, waits for them, and re-layouts  7.86 us
    ppermute x3, starting transfers between devices, extended(): lax.ppermute(tail, axis, [(i, (i + 1) % count) for i in range(count)])  4.78 us
    add_any x1, other arithmetic, edge_messages(): separation = far_rows[:, :, :3] - owned_places[None]  4.4 us
    add_any x2, other arithmetic, edge_messages(): path_weights[:, :, 0] * far_scalars + path_weights[:, :, 1] * projected  3.87 us
  transfers between devices with their start and end apart: 12, of which 9 were waited for; matrix products, arithmetic and copies ran while one was open for 2% of the time, Pallas kernels for 0%

commit v1 on v0

v1 whole, which is shorter than its diff:
```python
import functools

import jax
import jax.numpy as jnp
from jax import lax
from jax.experimental import pallas as pl
from jax.experimental.pallas import tpu as pltpu
from jax.sharding import PartitionSpec as P

SOFTENING = 0.25
SHARPNESS = 2.0
FIRST_CENTRE = 0.5
SPACING = 0.4
EDGE = 1.0

MESH = pl.DeviceIdType.MESH
HIGHEST = lax.Precision.HIGHEST
NT = (((1,), (1,)), ((), ()))

OWN, NEAR, FAR = 9, 12, 15
SELF = 10
RAW = 27


def sigmoid(x):
    return 1.0 / (1.0 + jnp.exp(-x))


def column(row):
    n = row.shape[1]
    eye = lax.broadcasted_iota(jnp.int32, (n, n), 0) == lax.broadcasted_iota(jnp.int32, (n, n), 1)
    return jnp.sum(jnp.where(eye, jnp.broadcast_to(row, (n, n)), 0.0), axis=1, keepdims=True)


def row_of(col):
    n = col.shape[0]
    eye = lax.broadcasted_iota(jnp.int32, (n, n), 0) == lax.broadcasted_iota(jnp.int32, (n, n), 1)
    return jnp.sum(jnp.where(eye, jnp.broadcast_to(col, (n, n)), 0.0), axis=0, keepdims=True)


def kernel(
    sizes,
    count_ref,
    places_ref,
    scalars_ref,
    vectors_ref,
    species_ref,
    bound_ref,
    ids_ref,
    ncount_ref,
    first_ref,
    second_ref,
    third_ref,
    energy_table_ref,
    gains_ref,
    energy_ref,
    forces_ref,
    gscal_ref,
    gvec_ref,
    table,
    grads,
    from_z,
    from_x,
    from_y,
    hot,
    hot_t,
    far,
    weights,
    units,
    turn,
    edge_grads,
    weight_grads,
    send_sem,
    recv_sem,
    back_send,
    back_recv,
):
    nx, ny, nz = sizes
    atoms, channels = scalars_ref.shape
    slots = ids_ref.shape[1]
    edges = slots * atoms
    width = 4 * channels
    gx, gy, gz = lax.axis_index("gx"), lax.axis_index("gy"), lax.axis_index("gz")
    odd = lax.rem(gx, 2)
    sign = 1 - 2 * odd
    near = gx + sign
    ahead = lax.rem(gx + 2 * sign + nx, nx)
    behind = lax.rem(gx - 2 * sign + nx, nx)
    up, down = lax.rem(gy + 1, ny), lax.rem(gy + ny - 1, ny)
    right, left = lax.rem(gz + 1, nz), lax.rem(gz + nz - 1, nz)

    barrier = pltpu.get_barrier_semaphore()
    partners = [
        (near, down, gz),
        (near, gy, gz),
        (near, up, gz),
        (gx, down, gz),
        (gx, up, gz),
        (ahead, gy, gz),
        (behind, gy, gz),
        (gx, gy, left),
        (gx, gy, right),
    ]
    for partner in partners:
        pl.semaphore_signal(barrier, inc=1, device_id=partner, device_id_type=MESH)

    lane = lax.broadcasted_iota(jnp.int32, (atoms, 128), 1)
    sub = lax.broadcasted_iota(jnp.int32, (atoms, 1), 0)
    own_places = jnp.zeros((atoms, 128), jnp.float32)
    for a in range(3):
        own_places = jnp.where(lane == a, column(places_ref[a : a + 1, :]), own_places)
    table[RAW, :, 0:channels] = scalars_ref[...]
    for a in range(3):
        table[RAW, :, (a + 1) * channels : (a + 2) * channels] = vectors_ref[a]
    table[RAW, :, width:] = own_places
    bound = column(bound_ref[...].astype(jnp.float32))
    alive = sub < count_ref[0]
    picks = [(bound == float(i)) & alive for i in range(atoms)]
    for c in range(0, width + 128, 128):
        block = table[RAW, :, c : c + 128]
        packet = jnp.zeros((atoms, 128), jnp.float32)
        for i in range(atoms):
            packet = jnp.where(picks[i], block[i : i + 1, :], packet)
        table[SELF, :, c : c + 128] = packet

    pl.semaphore_wait(barrier, len(partners))

    def copy(index, source, target, partner, sems=(send_sem, recv_sem)):
        made = pltpu.make_async_remote_copy(
            src_ref=source,
            dst_ref=target,
            send_sem=sems[0].at[index],
            recv_sem=sems[1].at[index],
            device_id=partner,
            device_id_type=MESH,
        )
        made.start()
        return made

    def blocks(ref, start, count=3):
        return ref.at[pl.ds(start, count)]

    sends = []
    to_near = [
        copy(2 + n, blocks(table, SELF, 1), blocks(table, NEAR + n, 1), (near, place, gz))
        for n, place in ((0, up), (1, gy), (2, down))
    ]
    to_side = [
        copy(0, blocks(table, SELF, 1), blocks(table, OWN, 1), (gx, up, gz)),
        copy(1, blocks(table, SELF, 1), blocks(table, OWN + 2, 1), (gx, down, gz)),
    ]

    ids = ids_ref[...]
    ghost = jnp.maximum(ids - atoms, 0)
    t = lax.shift_right_logical(ghost, 3)
    one = lambda test: jnp.where(test, 1, 0)
    ox = one(t >= 9) + one(t >= 18) - 1
    rest = t - 9 * (ox + 1)
    oy = one(rest >= 3) + one(rest >= 6) - 1
    oz = rest - 3 * (oy + 1) - 1
    group = jnp.where(ox == 0, 0, jnp.where(ox == sign, 1, 2))
    mapped = 8 * (9 * (oz + 1) + 3 * group + (oy + 1)) + (ghost & 7)
    mapped = jnp.where(ids < atoms, 8 * RAW + ids, mapped)
    rows = 8 * (RAW + 1)
    row_iota = lax.broadcasted_iota(jnp.int32, (atoms, rows), 1)
    hot_f32 = jnp.concatenate(
        [jnp.where(mapped[:, k : k + 1] == row_iota, 1.0, 0.0) for k in range(slots)], axis=0
    )
    hot[...] = hot_f32
    hot_t[...] = hot_f32.T

    for made in to_side:
        made.wait()
    sends.append(copy(6, blocks(table, OWN), blocks(table, 0), (gx, gy, right)))
    sends.append(copy(7, blocks(table, OWN), blocks(table, 18), (gx, gy, left)))
    for made in to_near:
        made.wait()
    ahead_copy = copy(5, blocks(table, NEAR), blocks(table, FAR), (ahead, gy, gz))
    sends.append(copy(8, blocks(table, NEAR), blocks(table, 3), (gx, gy, right)))
    sends.append(copy(9, blocks(table, NEAR), blocks(table, 21), (gx, gy, left)))
    ahead_copy.wait()
    sends.append(copy(10, blocks(table, FAR), blocks(table, 6), (gx, gy, right)))
    sends.append(copy(11, blocks(table, FAR), blocks(table, 24), (gx, gy, left)))
    for made in sends:
        made.wait()

    fsign = sign.astype(jnp.float32)
    unit = [jnp.where(lane == a, EDGE, 0.0) for a in range(3)]
    moved = []
    for z in (-1.0, 0.0, 1.0):
        for g in (0.0, fsign, -fsign):
            for y in (-1.0, 0.0, 1.0):
                moved.append(unit[0] * g + unit[1] * y + unit[2] * z)
    moved.append(jnp.zeros((atoms, 128), jnp.float32))
    positions = jnp.concatenate(
        [table[n, :, width:] + moved[n] for n in range(RAW + 1)], axis=0
    )
    picked = jnp.dot(hot[...], positions, precision=HIGHEST, preferred_element_type=jnp.float32)
    apart = picked.reshape(slots, atoms, 128) - own_places[None]
    distance = jnp.sqrt(jnp.sum(apart * apart, axis=2, keepdims=True) + SOFTENING)
    inverse = 1.0 / distance
    for a in range(3):
        units[a] = jnp.broadcast_to(apart[:, :, a : a + 1] * inverse, (slots, atoms, 128))
    distance = distance.reshape(edges, 1)
    gaussians = first_ref.shape[0]
    centres = FIRST_CENTRE + SPACING * lax.broadcasted_iota(
        jnp.int32, (edges, gaussians), 1
    ).astype(jnp.float32)
    gap = distance - centres
    gauss = jnp.exp(-SHARPNESS * gap * gap)
    pre_one = jnp.dot(
        gauss.astype(jnp.bfloat16), first_ref[...], preferred_element_type=jnp.float32
    )
    gate_one = sigmoid(pre_one)
    hidden_one = (pre_one * gate_one).astype(jnp.bfloat16)
    pre_two = jnp.dot(hidden_one, second_ref[...], preferred_element_type=jnp.float32)
    gate_two = sigmoid(pre_two)
    ncount = column(ncount_ref[...].astype(jnp.float32))
    listed = jnp.concatenate(
        [jnp.where(ncount > float(k), 1.0, 0.0) for k in range(slots)], axis=0
    )
    hidden_two = (pre_two * gate_two * listed).astype(jnp.bfloat16)
    weights[...] = jnp.dot(
        hidden_two, third_ref[...], preferred_element_type=jnp.float32
    ).reshape(slots, atoms, 6 * channels)

    features = table[:, :, 0:width].reshape(rows, width).astype(jnp.bfloat16)
    far[...] = jnp.dot(
        hot[...].astype(jnp.bfloat16), features, preferred_element_type=jnp.float32
    ).reshape(slots, atoms, width)

    step = 2
    scale = slots ** (-0.5)
    quarter = channels ** (-0.25)
    species = column(species_ref[...].astype(jnp.float32))
    energy = jnp.zeros((atoms, 1), jnp.float32)
    cotans = []
    halves = channels // 128

    def loads(ks, h):
        w = [weights[ks, :, n * channels + h * 128 : n * channels + h * 128 + 128] for n in range(6)]
        s = far[ks, :, h * 128 : h * 128 + 128]
        v = [
            far[ks, :, (a + 1) * channels + h * 128 : (a + 1) * channels + h * 128 + 128]
            for a in range(3)
        ]
        u = [units[a, ks] for a in range(3)]
        return w, s, v, u

    def cross(x, y):
        return [
            x[1] * y[2] - x[2] * y[1],
            x[2] * y[0] - x[0] * y[2],
            x[0] * y[1] - x[1] * y[0],
        ]

    def dot3(x, y):
        return x[0] * y[0] + x[1] * y[1] + x[2] * y[2]

    for h in range(halves):
        cut = slice(h * 128, h * 128 + 128)

        def forward(n, carry, h=h):
            ks = pl.ds(n * step, step)
            w, s, v, u = loads(ks, h)
            q = dot3(u, v)
            turned = cross(v, u)
            along = w[2] * s + w[5] * q
            straight = w[3] - w[5] * (1.0 / 3.0)
            out = [carry[0] + jnp.sum(w[0] * s + w[1] * q, axis=0)]
            for a in range(3):
                out.append(
                    carry[1 + a]
                    + jnp.sum(along * u[a] + straight * v[a] + w[4] * turned[a], axis=0)
                )
            return tuple(out)

        zero = jnp.zeros((atoms, 128), jnp.float32)
        sums = lax.fori_loop(0, slots // step, forward, (zero,) * 4)
        s_out = scalars_ref[:, cut] + scale * sums[0]
        v_out = [vectors_ref[a, :, cut] + scale * sums[1 + a] for a in range(3)]
        coeff = jnp.zeros((atoms, 128), jnp.float32)
        for z in range(energy_table_ref.shape[0]):
            coeff = jnp.where(species == float(z), energy_table_ref[z : z + 1, cut], coeff)
        gains = gains_ref[:, cut]
        gate = sigmoid(s_out)
        part = coeff * (s_out * gate) + gains * dot3(v_out, v_out)
        energy = energy + jnp.sum(part, axis=1, keepdims=True)
        cs = quarter * coeff * (gate * (1.0 + s_out * (1.0 - gate)))
        cv = [(2.0 * quarter) * gains * v for v in v_out]
        cotans.append((cs, cv))
    energy_ref[...] = row_of(energy * quarter)

    for h in range(halves):
        cs, cv = cotans[h]
        gs = (scale * cs)[None]
        gv = [(scale * c)[None] for c in cv]

        def backward(n, carry, h=h, gs=gs, gv=gv):
            ks = pl.ds(n * step, step)
            row = pl.ds(pl.multiple_of(n * step * atoms, step * atoms), step * atoms)
            w, s, v, u = loads(ks, h)
            q = dot3(u, v)
            turned = cross(v, u)
            p = dot3(gv, u)
            same = dot3(gv, v)

            def put(ref, block, value):
                ref[row, block * channels + h * 128 : block * channels + h * 128 + 128] = (
                    value.reshape(step * atoms, 128).astype(jnp.bfloat16)
                )

            put(weight_grads, 0, gs * s)
            put(weight_grads, 1, gs * q)
            put(weight_grads, 2, s * p)
            put(weight_grads, 3, same)
            put(weight_grads, 4, dot3(gv, turned))
            put(weight_grads, 5, p * q - same * (1.0 / 3.0))
            dq = w[1] * gs + w[5] * p
            straight = w[3] - w[5] * (1.0 / 3.0)
            put(edge_grads, 0, w[0] * gs + w[2] * p)
            back = cross(u, gv)
            along = w[2] * s + w[5] * q
            spun = cross(gv, v)
            for a in range(3):
                put(edge_grads, 1 + a, dq * u[a] + straight * gv[a] + w[4] * back[a])
                piece = dq * v[a] + along * gv[a] + w[4] * spun[a]
                if h == 0:
                    turn[a, ks] = piece
                else:
                    turn[a, ks] += piece
            return carry

        lax.fori_loop(0, slots // step, backward, 0)

    summed = jnp.dot(
        hot_t[...].astype(jnp.bfloat16), edge_grads[...], preferred_element_type=jnp.float32
    )
    grads[:, :, 0:width] = summed.reshape(RAW + 1, atoms, width)

    d_two = lax.dot_general(
        weight_grads[...], third_ref[...], NT, preferred_element_type=jnp.float32
    )
    d_two = d_two * listed * (gate_two * (1.0 + pre_two * (1.0 - gate_two)))
    d_one = lax.dot_general(
        d_two.astype(jnp.bfloat16), second_ref[...], NT, preferred_element_type=jnp.float32
    )
    d_one = d_one * (gate_one * (1.0 + pre_one * (1.0 - gate_one)))
    d_gauss = lax.dot_general(
        d_one.astype(jnp.bfloat16), first_ref[...], NT, preferred_element_type=jnp.float32
    )
    d_distance = jnp.sum(
        d_gauss * gauss * gap * (-2.0 * SHARPNESS), axis=1, keepdims=True
    ).reshape(slots, atoms, 1)
    d_unit = [jnp.sum(turn[a], axis=2, keepdims=True) for a in range(3)]
    u = [units[a, :, :, 0:1] for a in range(3)]
    radial = d_distance - dot3(d_unit, u) * inverse
    lanes = lax.broadcasted_iota(jnp.int32, (slots, atoms, 128), 2)
    d_apart = jnp.zeros((slots, atoms, 128), jnp.float32)
    for a in range(3):
        d_apart = jnp.where(lanes == a, d_unit[a] * inverse + radial * u[a], d_apart)
    pulled = jnp.dot(
        hot_t[...],
        d_apart.reshape(edges, 128),
        precision=HIGHEST,
        preferred_element_type=jnp.float32,
    )
    grads[:, :, width:] = pulled.reshape(RAW + 1, atoms, 128)

    back = (back_send, back_recv)
    returns = []
    for g in (2, 1, 0):
        returns.append(
            (
                copy(6 + 2 * g, blocks(grads, 3 * g), blocks(from_z, 3 * g), (gx, gy, left), back),
                copy(
                    7 + 2 * g,
                    blocks(grads, 18 + 3 * g),
                    blocks(from_z, 9 + 3 * g),
                    (gx, gy, right),
                    back,
                ),
            )
        )
    pending = []

    def fold(g):
        for made in returns[2 - g]:
            made.wait()
        total = grads[OWN + 3 * g : OWN + 3 * g + 3]
        return total + from_z[3 * g : 3 * g + 3] + from_z[9 + 3 * g : 12 + 3 * g]

    grads[FAR : FAR + 3] = fold(2)
    far_copy = copy(5, blocks(grads, FAR), blocks(from_x, 0), (behind, gy, gz), back)
    near_sum = fold(1)
    far_copy.wait()
    grads[NEAR : NEAR + 3] = near_sum + from_x[...]
    for n, place in ((0, down), (1, gy), (2, up)):
        pending.append(
            copy(
                2 + n,
                blocks(grads, NEAR + n, 1),
                blocks(from_y, 4 - n, 1),
                (near, place, gz),
                back,
            )
        )
    grads[OWN : OWN + 3] = fold(0)
    pending.append(copy(0, blocks(grads, OWN, 1), blocks(from_y, 0, 1), (gx, down, gz), back))
    pending.append(copy(1, blocks(grads, OWN + 2, 1), blocks(from_y, 1, 1), (gx, up, gz), back))
    for made in pending:
        made.wait()

    def final(c):
        cut = slice(c, c + 128)
        total = grads[SELF, :, cut]
        for n in range(5):
            total = total + from_y[n, :, cut]
        total = jnp.where(alive, total, 0.0)
        back_home = grads[RAW, :, cut]
        for b in range(atoms):
            back_home = back_home + jnp.where(homes[b], total[b : b + 1, :], 0.0)
        return back_home

    homes = [bound_ref[:, b : b + 1] == sub for b in range(atoms)]
    for h in range(halves):
        cs, cv = cotans[h]
        cut = slice(h * 128, h * 128 + 128)
        gscal_ref[:, cut] = final(h * 128) + cs
        for a in range(3):
            gvec_ref[a, :, cut] = final((a + 1) * channels + h * 128) + cv[a]
    pull = jnp.sum(d_apart, axis=0) - final(width)
    for a in range(3):
        forces_ref[a : a + 1, :] = row_of(pull[:, a : a + 1])


def shards(sizes):
    def run(
        places,
        scalars,
        vectors,
        species,
        bound_rows,
        bound_count,
        neighbour_ids,
        neighbour_count,
        radial_first,
        radial_second,
        radial_third,
        energy_table,
        vector_gains,
    ):
        atoms, channels = scalars.shape
        slots = neighbour_ids.shape[0]
        edges = slots * atoms
        packed = 4 * channels + 128
        vmem = pl.BlockSpec(memory_space=pltpu.VMEM)
        f32 = jnp.float32
        energies, forces, grad_scalars, grad_vectors = pl.pallas_call(
            functools.partial(kernel, sizes),
            out_shape=(
                jax.ShapeDtypeStruct((1, atoms), f32),
                jax.ShapeDtypeStruct((3, atoms), f32),
                jax.ShapeDtypeStruct((atoms, channels), f32),
                jax.ShapeDtypeStruct((3, atoms, channels), f32),
            ),
            in_specs=[pl.BlockSpec(memory_space=pltpu.SMEM)] + [vmem] * 12,
            out_specs=(vmem,) * 4,
            scratch_shapes=[
                pltpu.VMEM((RAW + 1, atoms, packed), f32),
                pltpu.VMEM((RAW + 1, atoms, packed), f32),
                pltpu.VMEM((18, atoms, packed), f32),
                pltpu.VMEM((3, atoms, packed), f32),
                pltpu.VMEM((5, atoms, packed), f32),
                pltpu.VMEM((edges, 8 * (RAW + 1)), f32),
                pltpu.VMEM((8 * (RAW + 1), edges), f32),
                pltpu.VMEM((slots, atoms, 4 * channels), f32),
                pltpu.VMEM((slots, atoms, 6 * channels), f32),
                pltpu.VMEM((3, slots, atoms, 128), f32),
                pltpu.VMEM((3, slots, atoms, 128), f32),
                pltpu.VMEM((edges, 4 * channels), jnp.bfloat16),
                pltpu.VMEM((edges, 6 * channels), jnp.bfloat16),
                pltpu.SemaphoreType.DMA((12,)),
                pltpu.SemaphoreType.DMA((12,)),
                pltpu.SemaphoreType.DMA((12,)),
                pltpu.SemaphoreType.DMA((12,)),
            ],
            compiler_params=pltpu.CompilerParams(
                collective_id=0, has_side_effects=True, vmem_limit_bytes=48 * 1024 * 1024
            ),
        )(
            bound_count,
            places.T,
            scalars,
            vectors.transpose(1, 0, 2),
            species.reshape(1, -1),
            bound_rows.reshape(1, -1),
            neighbour_ids.T,
            neighbour_count.reshape(1, -1),
            radial_first,
            radial_second,
            radial_third,
            energy_table,
            vector_gains.reshape(1, -1),
        )
        return energies.reshape(-1), forces.T, grad_scalars, grad_vectors.transpose(1, 0, 2)

    return run


def solution(mesh):
    spread = ("gx", "gy", "gz")
    in_specs = (
        P(spread, None),
        P(spread, None),
        P(spread, None, None),
        P(spread),
        P(spread),
        P(spread),
        P(None, spread),
        P(spread),
        P(),
        P(),
        P(),
        P(),
        P(),
    )
    out_specs = (P(spread), P(spread, None), P(spread, None), P(spread, None, None))
    sizes = tuple(mesh.shape[axis] for axis in spread)
    return jax.shard_map(
        shards(sizes), mesh=mesh, in_specs=in_specs, out_specs=out_specs, check_vma=False
    )
```

time: 170 us -> 56.6 us (0.33)
  Pallas kernels: 0 us -> 46.2 us
  starting transfers between devices: 44.2 us -> 0 us
  local copies, waits for them, and re-layouts: 50.9 us -> 8.69 us
  other arithmetic: 36.1 us -> 0 us
  waiting for transfers between devices: 31 us -> 0 us
  matrix products: 4.38 us -> 0 us
    pallas_call x0 -> x1, Pallas kernels: none -> 46.2 us  [run(): pl.pallas_call(functools.partial(kernel, sizes), out_shape=(jax.ShapeDtyp...]
    ppermute x12 -> x0, starting transfers between devices: 44.2 us -> none  [the longest x3 22 us: extended(): lax.ppermute(head, axis, [((i + 1) % count, i) for i in range(count)])]
    ppermute x12 -> x0, waiting for transfers between devices: 31 us -> none  [the longest x6 16.6 us: shifted(): lax.ppermute(value, axis, [(i, (i + by) % size) for i in range(size)])]
    reduce_sum x19 -> x0, local copies, waits for them, and re-layouts: 23.4 us -> none  [the longest x2 3.08 us: edge_messages(): path_weights[:, :, 2:3] * far_scalars[:, :, None] * direction[:, :, :, None]]
    add_any x4 -> x0, other arithmetic: 11.1 us -> none  [the longest x1 4.4 us: edge_messages(): separation = far_rows[:, :, :3] - owned_places[None]]
    mul x12 -> x0, other arithmetic: 9.25 us -> none  [the longest x1 2.61 us: edge_messages(): path_weights[:, :, 1] * projected]
    add_any x3 -> x0, local copies, waits for them, and re-layouts: 8.2 us -> none  [the longest x1 3.27 us: edge_messages(): separation = far_rows[:, :, :3] - owned_places[None]]
    reduce_sum x9 -> x0, other arithmetic: 7.98 us -> none  [the longest x1 3.24 us: edge_messages(): path_weights[:, :, 5:6]]
  transfers between devices with their start and end apart: 12 -> 0, of which waited for: 9 -> 0; matrix products, arithmetic and copies ran while one was open for 2% -> 0% of each run, Pallas kernels for 0% -> 0%
where the time goes in v1:
time: 56.6 us; the launch traced here: 56.2 us
  Pallas kernels  46.2 us (82%)
  local copies, waits for them, and re-layouts  8.69 us (15%)
  between operations  1.35 us (2%)
    pallas_call x1, Pallas kernels, run(): pl.pallas_call(functools.partial(kernel, sizes), out_shape=(jax.ShapeDtyp...  46.2 us
    unnamed x28, local copies, waits for them, and re-layouts  8.69 us

profile of v1, /device:TPU:7, one launch (start us, length us, event | category | flops | bytes accessed | tf_op | source)
XLA Modules:
  0.0 56.2 jit_solution(8004867736175035661)
XLA Ops:
  0.6 0.0 copy-start.3
  1.3 0.0 copy-start.4
  1.3 0.0 copy-start.6
  1.3 0.0 copy-start.8
  1.3 0.0 copy-done.3
  1.3 0.6 %copy-done.4 = s32[16,8]{0,1:T(8,128)S(1)} copy-done((s32[16,8]{0,1:T(8,128)S(1)}, s32[16,8]{0,1:T(8,128)}, u32[]{:S(2)}) %copy-start.4) | copy-done | bytes 536
  2.0 0.0 copy-done.6
  2.0 0.0 copy-done.8
  2.0 0.0 copy-start
  2.0 0.9 %copy-done = bf16[64,1536]{1,0:T(8,128)(2,1)S(1)} copy-done((bf16[64,1536]{1,0:T(8,128)(2,1)S(1)}, bf16[64,1536]{1,0:T(8,128)(2,1)}, u32[]{:S(2)}) %copy-start) | copy-done | bytes 196632
  2.9 0.0 copy-start.1
  2.9 0.7 %copy-done.1 = f32[8,3,256]{2,0,1:T(8,128)S(1)} copy-done((f32[8,3,256]{2,0,1:T(8,128)S(1)}, f32[8,3,256]{2,0,1:T(8,128)}, u32[]{:S(2)}) %copy-start.1) | copy-done | bytes 24600
  3.7 0.0 copy-start.2
  3.7 0.7 %copy-done.2 = bf16[64,64]{1,0:T(8,128)(2,1)S(1)} copy-done((bf16[64,64]{1,0:T(8,128)(2,1)S(1)}, bf16[64,64]{1,0:T(8,128)(2,1)}, u32[]{:S(2)}) %copy-start.2) | copy-done | bytes 8216
  4.4 0.0 copy-start.5
  4.4 0.7 %copy-done.5 = f32[4,256]{1,0:T(4,128)S(1)} copy-done((f32[4,256]{1,0:T(4,128)S(1)}, f32[4,256]{1,0:T(4,128)}, u32[]{:S(2)}) %copy-start.5) | copy-done | bytes 4120
  5.1 0.0 copy-start.7
  5.1 0.7 %copy-done.7 = bf16[8,64]{1,0:T(8,128)(2,1)S(1)} copy-done((bf16[8,64]{1,0:T(8,128)(2,1)S(1)}, bf16[8,64]{1,0:T(8,128)(2,1)}, u32[]{:S(2)}) %copy-start.7) | copy-done | bytes 1048
  5.8 0.0 copy-start.9
  5.8 0.7 %copy-done.9 = s32[8]{0:T(128)S(1)} copy-done((s32[8]{0:T(128)S(1)}, s32[8]{0:T(128)}, u32[]{:S(2)}) %copy-start.9) | copy-done | bytes 56
  6.4 0.0 copy-start.10
  6.4 0.7 %copy-done.10 = s32[8]{0:T(128)S(1)} copy-done((s32[8]{0:T(128)S(1)}, s32[8]{0:T(128)}, u32[]{:S(2)}) %copy-start.10) | copy-done | bytes 56
  7.1 0.0 copy-start.11
  7.1 0.7 %copy-done.11 = s32[8]{0:T(128)S(1)} copy-done((s32[8]{0:T(128)S(1)}, s32[8]{0:T(128)}, u32[]{:S(2)}) %copy-start.11) | copy-done | bytes 56
  7.7 46.2 %shard_map.156 = (f32[1,8]{1,0:T(1,128)S(1)}, f32[3,8]{1,0:T(4,128)S(1)}, f32[8,256]{1,0:T(8,128)S(1)}, f32[3,8,256]{2,1,0:T(8,128)S(1)}) custom-call(s32[1]{0:T(128)S(6)} %copy.21.count_ref, f32[3,8]{1,0:T(4,128)S(1)} %bitcast.13, f32[8,256]{1,0:T(8,128)S(1)} %copy-done.3, f32[3,8,256]{2,1,0:T(8,128)S(1)} %bitcast.10, s32[1,8]{1,0:T(1,128)S(1)} %bitcast.16, ...), custom_call_target="tpu_custom_call" | custom-call | tf_op jit(solution)/shard_map/pallas_call | solution.py:459
  53.9 0.5 copy.22
  54.4 0.6 %copy.23 = f32[8,3]{0,1:T(4,128)} copy(f32[8,3]{0,1:T(4,128)S(1)} %bitcast.14) | data formatting | bytes 192
  55.0 0.6 %copy.24 = f32[8,256]{1,0:T(8,128)} copy(f32[8,256]{1,0:T(8,128)S(1)} %get-tuple-element.18) | data formatting | bytes 16384
  55.6 0.6 %copy.25 = f32[8,3,256]{2,0,1:T(8,128)} copy(f32[8,3,256]{2,0,1:T(8,128)S(1)} %bitcast.11) | data formatting | bytes 49152
Async XLA Ops:
  0.6 0.7 %copy-start.3 = (f32[8,256]{1,0:T(8,128)S(1)}, f32[8,256]{1,0:T(8,128)}, u32[]{:S(2)}) copy-start(f32[8,256]{1,0:T(8,128)} %scalars_ref.1) | copy-start | bytes 24580
  1.3 0.7 %copy-start.4 = (s32[16,8]{0,1:T(8,128)S(1)}, s32[16,8]{0,1:T(8,128)}, u32[]{:S(2)}) copy-start(s32[16,8]{0,1:T(8,128)} %param.19) | copy-start | bytes 1540
  1.3 0.7 %copy-start.6 = (f32[8,3]{0,1:T(4,128)S(1)}, f32[8,3]{0,1:T(4,128)}, u32[]{:S(2)}) copy-start(f32[8,3]{0,1:T(4,128)} %param.13) | copy-start | bytes 292
  1.3 0.7 %copy-start.8 = (f32[256]{0:T(256)S(1)}, f32[256]{0:T(256)}, u32[]{:S(2)}) copy-start(f32[256]{0:T(256)} %param.25) | copy-start | bytes 3076
  2.0 0.9 %copy-start = (bf16[64,1536]{1,0:T(8,128)(2,1)S(1)}, bf16[64,1536]{1,0:T(8,128)(2,1)}, u32[]{:S(2)}) copy-start(bf16[64,1536]{1,0:T(8,128)(2,1)} %third_ref.1) | copy-start | bytes 589828
  2.9 0.7 %copy-start.1 = (f32[8,3,256]{2,0,1:T(8,128)S(1)}, f32[8,3,256]{2,0,1:T(8,128)}, u32[]{:S(2)}) copy-start(f32[8,3,256]{2,0,1:T(8,128)} %param.15) | copy-start | bytes 73732
  3.7 0.7 %copy-start.2 = (bf16[64,64]{1,0:T(8,128)(2,1)S(1)}, bf16[64,64]{1,0:T(8,128)(2,1)}, u32[]{:S(2)}) copy-start(bf16[64,64]{1,0:T(8,128)(2,1)} %second_ref.1) | copy-start | bytes 24580
  4.4 0.7 %copy-start.5 = (f32[4,256]{1,0:T(4,128)S(1)}, f32[4,256]{1,0:T(4,128)}, u32[]{:S(2)}) copy-start(f32[4,256]{1,0:T(4,128)} %energy_table_ref.1) | copy-start | bytes 12292
  5.1 0.7 %copy-start.7 = (bf16[8,64]{1,0:T(8,128)(2,1)S(1)}, bf16[8,64]{1,0:T(8,128)(2,1)}, u32[]{:S(2)}) copy-start(bf16[8,64]{1,0:T(8,128)(2,1)} %first_ref.1) | copy-start | bytes 3076
  5.8 0.7 %copy-start.9 = (s32[8]{0:T(128)S(1)}, s32[8]{0:T(128)}, u32[]{:S(2)}) copy-start(s32[8]{0:T(128)} %param.16) | copy-start | bytes 100
  6.4 0.7 %copy-start.10 = (s32[8]{0:T(128)S(1)}, s32[8]{0:T(128)}, u32[]{:S(2)}) copy-start(s32[8]{0:T(128)} %param.17) | copy-start | bytes 100
  7.1 0.7 %copy-start.11 = (s32[8]{0:T(128)S(1)}, s32[8]{0:T(128)}, u32[]{:S(2)}) copy-start(s32[8]{0:T(128)} %param.20) | copy-start | bytes 100

commit v2 on v1

--- a/solution.py
+++ b/solution.py
@@ -41,9 +41,23 @@
 def kernel(
     sizes,
     count_ref,
+    places_hbm,
+    scalars_hbm,
+    vectors_hbm,
+    species_hbm,
+    bound_hbm,
+    ids_hbm,
+    ncount_hbm,
+    first_hbm,
+    second_hbm,
+    third_hbm,
+    energy_table_hbm,
+    gains_hbm,
+    energy_ref,
+    forces_ref,
+    gscal_ref,
+    gvec_ref,
     places_ref,
-    scalars_ref,
-    vectors_ref,
     species_ref,
     bound_ref,
     ids_ref,
@@ -53,10 +67,7 @@
     third_ref,
     energy_table_ref,
     gains_ref,
-    energy_ref,
-    forces_ref,
-    gscal_ref,
-    gvec_ref,
+    load_sem,
     table,
     grads,
     from_z,
@@ -76,7 +87,7 @@
     back_recv,
 ):
     nx, ny, nz = sizes
-    atoms, channels = scalars_ref.shape
+    atoms, channels = scalars_hbm.shape
     slots = ids_ref.shape[1]
     edges = slots * atoms
     width = 4 * channels
@@ -104,14 +115,37 @@
     for partner in partners:
         pl.semaphore_signal(barrier, inc=1, device_id=partner, device_id_type=MESH)
 
+    loads_first = [
+        (scalars_hbm, table.at[RAW, :, pl.ds(0, channels)]),
+        (vectors_hbm.at[0], table.at[RAW, :, pl.ds(channels, channels)]),
+        (vectors_hbm.at[1], table.at[RAW, :, pl.ds(2 * channels, channels)]),
+        (vectors_hbm.at[2], table.at[RAW, :, pl.ds(3 * channels, channels)]),
+        (places_hbm, places_ref),
+        (bound_hbm, bound_ref),
+    ]
+    loads_later = [
+        (ids_hbm, ids_ref),
+        (first_hbm, first_ref),
+        (second_hbm, second_ref),
+        (third_hbm, third_ref),
+        (ncount_hbm, ncount_ref),
+        (species_hbm, species_ref),
+        (energy_table_hbm, energy_table_ref),
+        (gains_hbm, gains_ref),
+    ]
+    incoming = []
+    for n, (source, target) in enumerate(loads_first + loads_later):
+        made = pltpu.make_async_copy(source, target, load_sem.at[n])
+        made.start()
+        incoming.append(made)
+
+    for made in incoming[: len(loads_first)]:
+        made.wait()
     lane = lax.broadcasted_iota(jnp.int32, (atoms, 128), 1)
     sub = lax.broadcasted_iota(jnp.int32, (atoms, 1), 0)
     own_places = jnp.zeros((atoms, 128), jnp.float32)
     for a in range(3):
         own_places = jnp.where(lane == a, column(places_ref[a : a + 1, :]), own_places)
-    table[RAW, :, 0:channels] = scalars_ref[...]
-    for a in range(3):
-        table[RAW, :, (a + 1) * channels : (a + 2) * channels] = vectors_ref[a]
     table[RAW, :, width:] = own_places
     bound = column(bound_ref[...].astype(jnp.float32))
     alive = sub < count_ref[0]
@@ -149,6 +183,9 @@
         copy(0, blocks(table, SELF, 1), blocks(table, OWN, 1), (gx, up, gz)),
         copy(1, blocks(table, SELF, 1), blocks(table, OWN + 2, 1), (gx, down, gz)),
     ]
+
+    for made in incoming[len(loads_first) :]:
+        made.wait()
 
     ids = ids_ref[...]
     ghost = jnp.maximum(ids - atoms, 0)
@@ -277,8 +314,8 @@
 
         zero = jnp.zeros((atoms, 128), jnp.float32)
         sums = lax.fori_loop(0, slots // step, forward, (zero,) * 4)
-        s_out = scalars_ref[:, cut] + scale * sums[0]
-        v_out = [vectors_ref[a, :, cut] + scale * sums[1 + a] for a in range(3)]
+        s_out = table[RAW, :, cut] + scale * sums[0]
+        v_out = [table[RAW, :, (a + 1) * channels + h * 128 : (a + 1) * channels + h * 128 + 128] + scale * sums[1 + a] for a in range(3)]
         coeff = jnp.zeros((atoms, 128), jnp.float32)
         for z in range(energy_table_ref.shape[0]):
             coeff = jnp.where(species == float(z), energy_table_ref[z : z + 1, cut], coeff)
@@ -432,6 +469,18 @@
     pull = jnp.sum(d_apart, axis=0) - final(width)
     for a in range(3):
         forces_ref[a : a + 1, :] = row_of(pull[:, a : a + 1])
+
+
+def settle(*refs):
+    count = len(refs) // 2
+    sems = refs[-1]
+    made = [
+        pltpu.make_async_copy(refs[n], refs[count + n], sems.at[n]) for n in range(count)
+    ]
+    for m in made:
+        m.start()
+    for m in made:
+        m.wait()
 
 
 def shards(sizes):
@@ -455,18 +504,40 @@
         edges = slots * atoms
         packed = 4 * channels + 128
         vmem = pl.BlockSpec(memory_space=pltpu.VMEM)
+        hbm = pl.BlockSpec(memory_space=pl.ANY)
         f32 = jnp.float32
-        energies, forces, grad_scalars, grad_vectors = pl.pallas_call(
+        operands = (
+            bound_count,
+            places.T,
+            scalars,
+            vectors.transpose(1, 0, 2),
+            species.reshape(1, -1),
+            bound_rows.reshape(1, -1),
+            neighbour_ids.T,
+            neighbour_count.reshape(1, -1),
+            radial_first,
+            radial_second,
+            radial_third,
+            energy_table,
+            vector_gains.reshape(1, -1),
+        )
+        landing = [
+            pltpu.VMEM(x.shape, x.dtype) for n, x in enumerate(operands) if n not in (0, 2, 3)
+        ]
+        out_shape = (
+            jax.ShapeDtypeStruct((1, atoms), f32),
+            jax.ShapeDtypeStruct((3, atoms), f32),
+            jax.ShapeDtypeStruct((atoms, channels), f32),
+            jax.ShapeDtypeStruct((3, atoms, channels), f32),
+        )
+        results = pl.pallas_call(
             functools.partial(kernel, sizes),
-            out_shape=(
-                jax.ShapeDtypeStruct((1, atoms), f32),
-                jax.ShapeDtypeStruct((3, atoms), f32),
-                jax.ShapeDtypeStruct((atoms, channels), f32),
-                jax.ShapeDtypeStruct((3, atoms, channels), f32),
-            ),
-            in_specs=[pl.BlockSpec(memory_space=pltpu.SMEM)] + [vmem] * 12,
+            out_shape=out_shape,
+            in_specs=[pl.BlockSpec(memory_space=pltpu.SMEM)] + [hbm] * 12,
             out_specs=(vmem,) * 4,
-            scratch_shapes=[
+            scratch_shapes=landing
+            + [
+                pltpu.SemaphoreType.DMA((14,)),
                 pltpu.VMEM((RAW + 1, atoms, packed), f32),
                 pltpu.VMEM((RAW + 1, atoms, packed), f32),
                 pltpu.VMEM((18, atoms, packed), f32),
@@ -486,23 +557,17 @@
                 pltpu.SemaphoreType.DMA((12,)),
             ],
             compiler_params=pltpu.CompilerParams(
-                collective_id=0, has_side_effects=True, vmem_limit_bytes=48 * 1024 * 1024
+                collective_id=0, has_side_effects=True, vmem_limit_bytes=56 * 1024 * 1024
             ),
-        )(
-            bound_count,
-            places.T,
-            scalars,
-            vectors.transpose(1, 0, 2),
-            species.reshape(1, -1),
-            bound_rows.reshape(1, -1),
-            neighbour_ids.T,
-            neighbour_count.reshape(1, -1),
-            radial_first,
-            radial_second,
-            radial_third,
-            energy_table,
-            vector_gains.reshape(1, -1),
-        )
+        )(*operands)
+        energies, forces, grad_scalars, grad_vectors = pl.pallas_call(
+            settle,
+            out_shape=out_shape,
+            in_specs=[hbm] * 4,
+            out_specs=(hbm,) * 4,
+            scratch_shapes=[pltpu.SemaphoreType.DMA((4,))],
+            compiler_params=pltpu.CompilerParams(vmem_limit_bytes=56 * 1024 * 1024),
+        )(*results)
         return energies.reshape(-1), forces.T, grad_scalars, grad_vectors.transpose(1, 0, 2)
 
     return run

time: 56.6 us -> 50.5 us (0.89)
  local copies, waits for them, and re-layouts: 8.69 us -> 0 us
  Pallas kernels: 46.2 us -> 49.1 us
    unnamed x28 -> x0, local copies, waits for them, and re-layouts: 8.69 us -> none
    pallas_call x1 -> x2, Pallas kernels: 46.2 us -> 49.1 us  [the longest x1 46.9 us: run(): pl.pallas_call(functools.partial(kernel, sizes), out_shape=out_shape, in_...]
where the time goes in v2:
time: 50.5 us; the launch traced here: 50.4 us
  Pallas kernels  49.1 us (97%)
  between operations  1.29 us (3%)
    pallas_call x1, Pallas kernels, run(): pl.pallas_call(functools.partial(kernel, sizes), out_shape=out_shape, in_...  46.9 us
    pallas_call x1, Pallas kernels, run(): pl.pallas_call(settle, out_shape=out_shape, in_specs=[hbm] * 4, out_specs...  2.2 us

profile of v2, /device:TPU:7, one launch (start us, length us, event | category | flops | bytes accessed | tf_op | source)
XLA Modules:
  0.0 50.4 jit_solution(400787816102883927)
XLA Ops:
  1.3 46.9 %shard_map.156 = (f32[1,8]{1,0:T(1,128)}, f32[3,8]{1,0:T(4,128)}, f32[8,256]{1,0:T(8,128)}, f32[3,8,256]{2,1,0:T(8,128)}) custom-call(s32[1]{0:T(128)S(6)} %copy.17.count_ref, f32[3,8]{1,0:T(4,128)} %bitcast.12, f32[8,256]{1,0:T(8,128)} %scalars_hbm.1, f32[3,8,256]{2,1,0:T(8,128)} %bitcast.10, s32[1,8]{1,0:T(1,128)} %bitcast.14, s32[1,8]{1,0:T(1,128)} %bitcast.15, ...), custom_call_target="tpu_custom_call" | custom-call | tf_op jit(solution)/shard_map/pallas_call | solution.py:533
  48.2 2.2 %shard_map.157 = (f32[1,8]{1,0:T(1,128)}, f32[3,8]{1,0:T(4,128)}, f32[8,256]{1,0:T(8,128)}, f32[3,8,256]{2,1,0:T(8,128)}) custom-call(f32[1,8]{1,0:T(1,128)} %get-tuple-element.12.refs_0_, f32[3,8]{1,0:T(4,128)} %get-tuple-element.13.refs_1_, f32[8,256]{1,0:T(8,128)} %get-tuple-element.14.refs_2_, f32[3,8,256]{2,1,0:T(8,128)} %get-tuple-element.15.refs_3_), custom_call_target="tpu_custom_call" | custom-call | tf_op jit(solution)/shard_map/pallas_call | solution.py:563

commit v3 on v2

--- a/solution.py
+++ b/solution.py
@@ -72,6 +72,7 @@
     grads,
     from_z,
     from_x,
+    from_w,
     from_y,
     hot,
     hot_t,
@@ -85,6 +86,7 @@
     recv_sem,
     back_send,
     back_recv,
+    ready,
 ):
     nx, ny, nz = sizes
     atoms, channels = scalars_hbm.shape
@@ -100,20 +102,34 @@
     up, down = lax.rem(gy + 1, ny), lax.rem(gy + ny - 1, ny)
     right, left = lax.rem(gz + 1, nz), lax.rem(gz + nz - 1, nz)
 
+    first, last = gx == 0, gx == nx - 1
+    three = ((0, down), (1, gy), (2, up))
     barrier = pltpu.get_barrier_semaphore()
+
+    def hello(partner):
+        pl.semaphore_signal(barrier, inc=1, device_id=partner, device_id_type=MESH)
+
     partners = [
         (near, down, gz),
         (near, gy, gz),
         (near, up, gz),
         (gx, down, gz),
         (gx, up, gz),
-        (ahead, gy, gz),
-        (behind, gy, gz),
         (gx, gy, left),
         (gx, gy, right),
     ]
     for partner in partners:
-        pl.semaphore_signal(barrier, inc=1, device_id=partner, device_id_type=MESH)
+        hello(partner)
+    for other in (ahead, behind):
+
+        @pl.when(other > gx)
+        def _(other=other):
+            hello((other, gy, gz))
+
+    @pl.when(first)
+    def _():
+        for n, place in three:
+            hello((nx - 1, place, gz))
 
     loads_first = [
         (scalars_hbm, table.at[RAW, :, pl.ds(0, channels)]),
@@ -157,22 +173,37 @@
             packet = jnp.where(picks[i], block[i : i + 1, :], packet)
         table[SELF, :, c : c + 128] = packet
 
-    pl.semaphore_wait(barrier, len(partners))
-
-    def copy(index, source, target, partner, sems=(send_sem, recv_sem)):
-        made = pltpu.make_async_remote_copy(
+    place_z, top = lax.div(gx, 2), nx // 2 - 1
+    earlier = lax.div(place_z + top - 1, top) + lax.div(place_z, top)
+    pl.semaphore_wait(barrier, len(partners) + earlier + 3 * lax.div(gx, nx - 1))
+
+    def plan(index, source, target, partner, sems=(send_sem, recv_sem), landed=None):
+        return pltpu.make_async_remote_copy(
             src_ref=source,
             dst_ref=target,
             send_sem=sems[0].at[index],
-            recv_sem=sems[1].at[index],
+            recv_sem=sems[1].at[index if landed is None else landed],
             device_id=partner,
             device_id_type=MESH,
         )
+
+    def copy(*args):
+        made = plan(*args)
         made.start()
         return made
 
     def blocks(ref, start, count=3):
         return ref.at[pl.ds(start, count)]
+
+    direct = [
+        plan(12 + n, blocks(table, SELF, 1), blocks(table, FAR + 2 - n, 1), (0, place, gz), landed=5)
+        for n, place in three
+    ]
+
+    @pl.when(last)
+    def _():
+        for made in direct:
+            made.start()
 
     sends = []
     to_near = [
@@ -183,6 +214,14 @@
         copy(0, blocks(table, SELF, 1), blocks(table, OWN, 1), (gx, up, gz)),
         copy(1, blocks(table, SELF, 1), blocks(table, OWN + 2, 1), (gx, down, gz)),
     ]
+
+    @pl.when(ahead < gx)
+    def _():
+        pl.semaphore_signal(ready.at[1], inc=1, device_id=(ahead, gy, gz), device_id_type=MESH)
+
+    @pl.when(behind < gx)
+    def _():
+        pl.semaphore_signal(ready.at[0], inc=1, device_id=(behind, gy, gz), device_id_type=MESH)
 
     for made in incoming[len(loads_first) :]:
         made.wait()
@@ -212,14 +251,33 @@
     sends.append(copy(7, blocks(table, OWN), blocks(table, 18), (gx, gy, left)))
     for made in to_near:
         made.wait()
-    ahead_copy = copy(5, blocks(table, NEAR), blocks(table, FAR), (ahead, gy, gz))
+    ahead_copy = plan(5, blocks(table, NEAR), blocks(table, FAR), (ahead, gy, gz))
+
+    @pl.when(ahead > gx)
+    def _():
+        pl.semaphore_wait(ready.at[0], 1)
+
+    @pl.when(gx != nx - 2)
+    def _():
+        ahead_copy.start()
+
     sends.append(copy(8, blocks(table, NEAR), blocks(table, 3), (gx, gy, right)))
     sends.append(copy(9, blocks(table, NEAR), blocks(table, 21), (gx, gy, left)))
-    ahead_copy.wait()
+    ahead_copy.wait_recv()
     sends.append(copy(10, blocks(table, FAR), blocks(table, 6), (gx, gy, right)))
     sends.append(copy(11, blocks(table, FAR), blocks(table, 24), (gx, gy, left)))
     for made in sends:
         made.wait()
+
+    @pl.when(gx != nx - 2)
+    def _():
+        ahead_copy.wait_send()
+
+    @pl.when(last)
+    def _():
+        for made in direct:
+            made.wait_send()
+
 
     fsign = sign.astype(jnp.float32)
     unit = [jnp.where(lane == a, EDGE, 0.0) for a in range(3)]
@@ -428,10 +486,32 @@
         return total + from_z[3 * g : 3 * g + 3] + from_z[9 + 3 * g : 12 + 3 * g]
 
     grads[FAR : FAR + 3] = fold(2)
-    far_copy = copy(5, blocks(grads, FAR), blocks(from_x, 0), (behind, gy, gz), back)
-    near_sum = fold(1)
-    far_copy.wait()
-    grads[NEAR : NEAR + 3] = near_sum + from_x[...]
+    far_copy = plan(5, blocks(grads, FAR), blocks(from_x, 0), (behind, gy, gz), back)
+    direct_back = [
+        plan(12 + n, blocks(grads, FAR + n, 1), blocks(from_w, 2 - n, 1), (0, place, gz), back, 14 - n)
+        for n, place in three
+    ]
+
+    @pl.when(behind > gx)
+    def _():
+        pl.semaphore_wait(ready.at[1], 1)
+
+    @pl.when(gx != nx - 1)
+    def _():
+        far_copy.start()
+
+    @pl.when(last)
+    def _():
+        for made in direct_back:
+            made.start()
+
+    grads[NEAR : NEAR + 3] = fold(1)
+
+    @pl.when(gx != 1)
+    def _():
+        far_copy.wait_recv()
+        grads[NEAR : NEAR + 3] += from_x[...]
+
     for n, place in ((0, down), (1, gy), (2, up)):
         pending.append(
             copy(
@@ -447,6 +527,22 @@
     pending.append(copy(1, blocks(grads, OWN + 2, 1), blocks(from_y, 1, 1), (gx, up, gz), back))
     for made in pending:
         made.wait()
+
+    @pl.when(first)
+    def _():
+        for made in direct_back:
+            made.wait_recv()
+        grads[SELF] += from_w[0] + from_w[1] + from_w[2]
+
+    @pl.when(gx != nx - 1)
+    def _():
+        far_copy.wait_send()
+
+    @pl.when(last)
+    def _():
+        for made in direct_back:
+            made.wait_send()
+
 
     def final(c):
         cut = slice(c, c + 128)
@@ -542,6 +638,7 @@
                 pltpu.VMEM((RAW + 1, atoms, packed), f32),
                 pltpu.VMEM((18, atoms, packed), f32),
                 pltpu.VMEM((3, atoms, packed), f32),
+                pltpu.VMEM((3, atoms, packed), f32),
                 pltpu.VMEM((5, atoms, packed), f32),
                 pltpu.VMEM((edges, 8 * (RAW + 1)), f32),
                 pltpu.VMEM((8 * (RAW + 1), edges), f32),
@@ -551,10 +648,11 @@
                 pltpu.VMEM((3, slots, atoms, 128), f32),
                 pltpu.VMEM((edges, 4 * channels), jnp.bfloat16),
                 pltpu.VMEM((edges, 6 * channels), jnp.bfloat16),
-                pltpu.SemaphoreType.DMA((12,)),
-                pltpu.SemaphoreType.DMA((12,)),
-                pltpu.SemaphoreType.DMA((12,)),
-                pltpu.SemaphoreType.DMA((12,)),
+                pltpu.SemaphoreType.DMA((15,)),
+                pltpu.SemaphoreType.DMA((15,)),
+                pltpu.SemaphoreType.DMA((15,)),
+                pltpu.SemaphoreType.DMA((15,)),
+                pltpu.SemaphoreType.REGULAR((2,)),
             ],
             compiler_params=pltpu.CompilerParams(
                 collective_id=0, has_side_effects=True, vmem_limit_bytes=56 * 1024 * 1024

time: 50.5 us -> 48 us (0.950); the launches traced: 50.4 us -> 47.1 us
  Pallas kernels: 49.1 us -> 45.8 us
    pallas_call x1, Pallas kernels: 46.9 us -> 43.6 us  [run(): pl.pallas_call(functools.partial(kernel, sizes), out_shape=out_shape, in_...]
where the time goes in v3:
time: 48 us; the launch traced here: 47.1 us
  Pallas kernels  45.8 us (95%)
  between operations  1.29 us (3%)
    pallas_call x1, Pallas kernels, run(): pl.pallas_call(functools.partial(kernel, sizes), out_shape=out_shape, in_...  43.6 us
    pallas_call x1, Pallas kernels, run(): pl.pallas_call(settle, out_shape=out_shape, in_specs=[hbm] * 4, out_specs...  2.2 us

profile of v3, /device:TPU:7, one launch (start us, length us, event | category | flops | bytes accessed | tf_op | source)
XLA Modules:
  0.0 47.1 jit_solution(5459394688079513350)
XLA Ops:
  1.3 43.6 %shard_map.156 = (f32[1,8]{1,0:T(1,128)}, f32[3,8]{1,0:T(4,128)}, f32[8,256]{1,0:T(8,128)}, f32[3,8,256]{2,1,0:T(8,128)}) custom-call(s32[1]{0:T(128)S(6)} %copy.17.count_ref, f32[3,8]{1,0:T(4,128)} %bitcast.12, f32[8,256]{1,0:T(8,128)} %scalars_hbm.1, f32[3,8,256]{2,1,0:T(8,128)} %bitcast.10, s32[1,8]{1,0:T(1,128)} %bitcast.14, s32[1,8]{1,0:T(1,128)} %bitcast.15, ...), custom_call_target="tpu_custom_call" | custom-call | tf_op jit(solution)/shard_map/pallas_call | solution.py:629
  44.9 2.2 %shard_map.157 = (f32[1,8]{1,0:T(1,128)}, f32[3,8]{1,0:T(4,128)}, f32[8,256]{1,0:T(8,128)}, f32[3,8,256]{2,1,0:T(8,128)}) custom-call(f32[1,8]{1,0:T(1,128)} %get-tuple-element.12.refs_0_, f32[3,8]{1,0:T(4,128)} %get-tuple-element.13.refs_1_, f32[8,256]{1,0:T(8,128)} %get-tuple-element.14.refs_2_, f32[3,8,256]{2,1,0:T(8,128)} %get-tuple-element.15.refs_3_), custom_call_target="tpu_custom_call" | custom-call | tf_op jit(solution)/shard_map/pallas_call | solution.py:661

commit v4 on v3

--- a/solution.py
+++ b/solution.py
@@ -74,6 +74,12 @@
     from_x,
     from_w,
     from_y,
+    place_table,
+    place_grads,
+    place_z,
+    place_x,
+    place_w,
+    place_y,
     hot,
     hot_t,
     far,
@@ -162,27 +168,37 @@
     own_places = jnp.zeros((atoms, 128), jnp.float32)
     for a in range(3):
         own_places = jnp.where(lane == a, column(places_ref[a : a + 1, :]), own_places)
-    table[RAW, :, width:] = own_places
+    place_table[RAW] = own_places
     bound = column(bound_ref[...].astype(jnp.float32))
     alive = sub < count_ref[0]
     picks = [(bound == float(i)) & alive for i in range(atoms)]
-    for c in range(0, width + 128, 128):
-        block = table[RAW, :, c : c + 128]
+
+
+    def packed(block):
         packet = jnp.zeros((atoms, 128), jnp.float32)
         for i in range(atoms):
             packet = jnp.where(picks[i], block[i : i + 1, :], packet)
-        table[SELF, :, c : c + 128] = packet
-
-    place_z, top = lax.div(gx, 2), nx // 2 - 1
-    earlier = lax.div(place_z + top - 1, top) + lax.div(place_z, top)
+        return packet
+
+    place_table[SELF] = packed(own_places)
+    for c in range(0, width, 128):
+        table[SELF, :, c : c + 128] = packed(table[RAW, :, c : c + 128])
+
+    level, top = lax.div(gx, 2), nx // 2 - 1
+    earlier = lax.div(level + top - 1, top) + lax.div(level, top)
     pl.semaphore_wait(barrier, len(partners) + earlier + 3 * lax.div(gx, nx - 1))
 
-    def plan(index, source, target, partner, sems=(send_sem, recv_sem), landed=None):
+    features = (0, table, grads, from_z, from_x, from_w, from_y)
+    positions = (16, place_table, place_grads, place_z, place_x, place_w, place_y)
+
+    def plan(kind, index, source, target, partner, sems=(send_sem, recv_sem), landed=None):
+        (source_ref, start, count), (target_ref, place) = source, target
+        landed = index if landed is None else landed
         return pltpu.make_async_remote_copy(
-            src_ref=source,
-            dst_ref=target,
-            send_sem=sems[0].at[index],
-            recv_sem=sems[1].at[index if landed is None else landed],
+            src_ref=kind[source_ref].at[pl.ds(start, count)],
+            dst_ref=kind[target_ref].at[pl.ds(place, count)],
+            send_sem=sems[0].at[kind[0] + index],
+            recv_sem=sems[1].at[kind[0] + landed],
             device_id=partner,
             device_id_type=MESH,
         )
@@ -192,28 +208,30 @@
         made.start()
         return made
 
-    def blocks(ref, start, count=3):
-        return ref.at[pl.ds(start, count)]
-
-    direct = [
-        plan(12 + n, blocks(table, SELF, 1), blocks(table, FAR + 2 - n, 1), (0, place, gz), landed=5)
-        for n, place in three
-    ]
+    direct = {
+        kind[0]: [
+            plan(kind, 12 + n, (1, SELF, 1), (1, FAR + 2 - n), (0, place, gz), landed=5)
+            for n, place in three
+        ]
+        for kind in (positions, features)
+    }
 
     @pl.when(last)
     def _():
-        for made in direct:
+        for made in direct[16] + direct[0]:
             made.start()
 
-    sends = []
-    to_near = [
-        copy(2 + n, blocks(table, SELF, 1), blocks(table, NEAR + n, 1), (near, place, gz))
-        for n, place in ((0, up), (1, gy), (2, down))
-    ]
-    to_side = [
-        copy(0, blocks(table, SELF, 1), blocks(table, OWN, 1), (gx, up, gz)),
-        copy(1, blocks(table, SELF, 1), blocks(table, OWN + 2, 1), (gx, down, gz)),
-    ]
+    sends = {0: [], 16: []}
+    to_near, to_side = {}, {}
+    for kind in (positions, features):
+        to_near[kind[0]] = [
+            copy(kind, 2 + n, (1, SELF, 1), (1, NEAR + n), (near, place, gz))
+            for n, place in ((0, up), (1, gy), (2, down))
+        ]
+        to_side[kind[0]] = [
+            copy(kind, 0, (1, SELF, 1), (1, OWN), (gx, up, gz)),
+            copy(kind, 1, (1, SELF, 1), (1, OWN + 2), (gx, down, gz)),
+        ]
 
     @pl.when(ahead < gx)
     def _():
@@ -245,39 +263,37 @@
     hot[...] = hot_f32
     hot_t[...] = hot_f32.T
 
-    for made in to_side:
+    def along_z(kind, g):
+        sends[kind[0]] += [
+            copy(kind, 6 + 2 * g, (1, OWN + 3 * g, 3), (1, 3 * g), (gx, gy, right)),
+            copy(kind, 7 + 2 * g, (1, OWN + 3 * g, 3), (1, 18 + 3 * g), (gx, gy, left)),
+        ]
+
+    for kind in (positions, features):
+        for made in to_side[kind[0]]:
+            made.wait()
+        along_z(kind, 0)
+
+    @pl.when(ahead > gx)
+    def _():
+        pl.semaphore_wait(ready.at[0], 1)
+
+    ahead_copy = {}
+    for kind in (positions, features):
+        for made in to_near[kind[0]]:
+            made.wait()
+        ahead_copy[kind[0]] = plan(kind, 5, (1, NEAR, 3), (1, FAR), (ahead, gy, gz))
+
+        @pl.when(gx != nx - 2)
+        def _(made=ahead_copy[kind[0]]):
+            made.start()
+
+        along_z(kind, 1)
+    for kind in (positions, features):
+        ahead_copy[kind[0]].wait_recv()
+        along_z(kind, 2)
+    for made in sends[16]:
         made.wait()
-    sends.append(copy(6, blocks(table, OWN), blocks(table, 0), (gx, gy, right)))
-    sends.append(copy(7, blocks(table, OWN), blocks(table, 18), (gx, gy, left)))
-    for made in to_near:
-        made.wait()
-    ahead_copy = plan(5, blocks(table, NEAR), blocks(table, FAR), (ahead, gy, gz))
-
-    @pl.when(ahead > gx)
-    def _():
-        pl.semaphore_wait(ready.at[0], 1)
-
-    @pl.when(gx != nx - 2)
-    def _():
-        ahead_copy.start()
-
-    sends.append(copy(8, blocks(table, NEAR), blocks(table, 3), (gx, gy, right)))
-    sends.append(copy(9, blocks(table, NEAR), blocks(table, 21), (gx, gy, left)))
-    ahead_copy.wait_recv()
-    sends.append(copy(10, blocks(table, FAR), blocks(table, 6), (gx, gy, right)))
-    sends.append(copy(11, blocks(table, FAR), blocks(table, 24), (gx, gy, left)))
-    for made in sends:
-        made.wait()
-
-    @pl.when(gx != nx - 2)
-    def _():
-        ahead_copy.wait_send()
-
-    @pl.when(last)
-    def _():
-        for made in direct:
-            made.wait_send()
-
 
     fsign = sign.astype(jnp.float32)
     unit = [jnp.where(lane == a, EDGE, 0.0) for a in range(3)]
@@ -287,10 +303,10 @@
             for y in (-1.0, 0.0, 1.0):
                 moved.append(unit[0] * g + unit[1] * y + unit[2] * z)
     moved.append(jnp.zeros((atoms, 128), jnp.float32))
-    positions = jnp.concatenate(
-        [table[n, :, width:] + moved[n] for n in range(RAW + 1)], axis=0
-    )
-    picked = jnp.dot(hot[...], positions, precision=HIGHEST, preferred_element_type=jnp.float32)
+    spots = jnp.concatenate(
+        [place_table[n] + moved[n] for n in range(RAW + 1)], axis=0
+    )
+    picked = jnp.dot(hot[...], spots, precision=HIGHEST, preferred_element_type=jnp.float32)
     apart = picked.reshape(slots, atoms, 128) - own_places[None]
     distance = jnp.sqrt(jnp.sum(apart * apart, axis=2, keepdims=True) + SOFTENING)
     inverse = 1.0 / distance
@@ -319,9 +335,22 @@
         hidden_two, third_ref[...], preferred_element_type=jnp.float32
     ).reshape(slots, atoms, 6 * channels)
 
-    features = table[:, :, 0:width].reshape(rows, width).astype(jnp.bfloat16)
+    for made in sends[0]:
+        made.wait()
+
+    @pl.when(gx != nx - 2)
+    def _():
+        for kind in (positions, features):
+            ahead_copy[kind[0]].wait_send()
+
+    @pl.when(last)
+    def _():
+        for made in direct[16] + direct[0]:
+            made.wait_send()
+
+    table_rows = table[...].reshape(rows, width).astype(jnp.bfloat16)
     far[...] = jnp.dot(
-        hot[...].astype(jnp.bfloat16), features, preferred_element_type=jnp.float32
+        hot[...].astype(jnp.bfloat16), table_rows, preferred_element_type=jnp.float32
     ).reshape(slots, atoms, width)
 
     step = 2
@@ -431,7 +460,20 @@
     summed = jnp.dot(
         hot_t[...].astype(jnp.bfloat16), edge_grads[...], preferred_element_type=jnp.float32
     )
-    grads[:, :, 0:width] = summed.reshape(RAW + 1, atoms, width)
+    grads[...] = summed.reshape(RAW + 1, atoms, width)
+
+    back = (back_send, back_recv)
+
+    def return_z(kind):
+        return [
+            [
+                copy(kind, 6 + 2 * g, (2, 3 * g, 3), (3, 3 * g), (gx, gy, left), back),
+                copy(kind, 7 + 2 * g, (2, 18 + 3 * g, 3), (3, 9 + 3 * g), (gx, gy, right), back),
+            ]
+            for g in (2, 1, 0)
+        ]
+
+    returns = {0: return_z(features)}
 
     d_two = lax.dot_general(
         weight_grads[...], third_ref[...], NT, preferred_element_type=jnp.float32
@@ -460,97 +502,79 @@
         precision=HIGHEST,
         preferred_element_type=jnp.float32,
     )
-    grads[:, :, width:] = pulled.reshape(RAW + 1, atoms, 128)
-
-    back = (back_send, back_recv)
-    returns = []
-    for g in (2, 1, 0):
-        returns.append(
-            (
-                copy(6 + 2 * g, blocks(grads, 3 * g), blocks(from_z, 3 * g), (gx, gy, left), back),
-                copy(
-                    7 + 2 * g,
-                    blocks(grads, 18 + 3 * g),
-                    blocks(from_z, 9 + 3 * g),
-                    (gx, gy, right),
-                    back,
-                ),
-            )
-        )
+    place_grads[...] = pulled.reshape(RAW + 1, atoms, 128)
+    returns[16] = return_z(positions)
+
     pending = []
 
-    def fold(g):
-        for made in returns[2 - g]:
+    def fold(kind, g):
+        for made in returns[kind[0]][2 - g]:
             made.wait()
-        total = grads[OWN + 3 * g : OWN + 3 * g + 3]
-        return total + from_z[3 * g : 3 * g + 3] + from_z[9 + 3 * g : 12 + 3 * g]
-
-    grads[FAR : FAR + 3] = fold(2)
-    far_copy = plan(5, blocks(grads, FAR), blocks(from_x, 0), (behind, gy, gz), back)
-    direct_back = [
-        plan(12 + n, blocks(grads, FAR + n, 1), blocks(from_w, 2 - n, 1), (0, place, gz), back, 14 - n)
-        for n, place in three
-    ]
+        span, came = pl.ds(OWN + 3 * g, 3), kind[3]
+        kind[2][span] += came[3 * g : 3 * g + 3] + came[9 + 3 * g : 12 + 3 * g]
 
     @pl.when(behind > gx)
     def _():
         pl.semaphore_wait(ready.at[1], 1)
 
-    @pl.when(gx != nx - 1)
-    def _():
-        far_copy.start()
-
-    @pl.when(last)
-    def _():
-        for made in direct_back:
+    far_copy, direct_back = {}, {}
+    for kind in (features, positions):
+        fold(kind, 2)
+        far_copy[kind[0]] = plan(kind, 5, (2, FAR, 3), (4, 0), (behind, gy, gz), back)
+        direct_back[kind[0]] = [
+            plan(kind, 12 + n, (2, FAR + n, 1), (5, 2 - n), (0, place, gz), back, 14 - n)
+            for n, place in three
+        ]
+
+        @pl.when(gx != nx - 1)
+        def _(made=far_copy[kind[0]]):
             made.start()
 
-    grads[NEAR : NEAR + 3] = fold(1)
-
-    @pl.when(gx != 1)
-    def _():
-        far_copy.wait_recv()
-        grads[NEAR : NEAR + 3] += from_x[...]
-
-    for n, place in ((0, down), (1, gy), (2, up)):
-        pending.append(
-            copy(
-                2 + n,
-                blocks(grads, NEAR + n, 1),
-                blocks(from_y, 4 - n, 1),
-                (near, place, gz),
-                back,
-            )
-        )
-    grads[OWN : OWN + 3] = fold(0)
-    pending.append(copy(0, blocks(grads, OWN, 1), blocks(from_y, 0, 1), (gx, down, gz), back))
-    pending.append(copy(1, blocks(grads, OWN + 2, 1), blocks(from_y, 1, 1), (gx, up, gz), back))
+        @pl.when(last)
+        def _(several=direct_back[kind[0]]):
+            for made in several:
+                made.start()
+
+    for kind in (features, positions):
+        fold(kind, 0)
+        pending.append(copy(kind, 0, (2, OWN, 1), (6, 0), (gx, down, gz), back))
+        pending.append(copy(kind, 1, (2, OWN + 2, 1), (6, 1), (gx, up, gz), back))
+        fold(kind, 1)
+    for kind in (features, positions):
+        @pl.when(gx != 1)
+        def _(kind=kind):
+            far_copy[kind[0]].wait_recv()
+            kind[2][NEAR : NEAR + 3] += kind[4][...]
+
+        for n, place in ((0, down), (1, gy), (2, up)):
+            pending.append(copy(kind, 2 + n, (2, NEAR + n, 1), (6, 4 - n), (near, place, gz), back))
     for made in pending:
         made.wait()
 
     @pl.when(first)
     def _():
-        for made in direct_back:
-            made.wait_recv()
-        grads[SELF] += from_w[0] + from_w[1] + from_w[2]
+        for kind in (features, positions):
+            for made in direct_back[kind[0]]:
+                made.wait_recv()
+            kind[2][SELF] += kind[5][0] + kind[5][1] + kind[5][2]
 
     @pl.when(gx != nx - 1)
     def _():
-        far_copy.wait_send()
+        for kind in (features, positions):
+            far_copy[kind[0]].wait_send()
 
     @pl.when(last)
     def _():
-        for made in direct_back:
+        for made in direct_back[0] + direct_back[16]:
             made.wait_send()
 
-
-    def final(c):
+    def final(kind, c):
         cut = slice(c, c + 128)
-        total = grads[SELF, :, cut]
+        total = kind[2][SELF, :, cut]
         for n in range(5):
-            total = total + from_y[n, :, cut]
+            total = total + kind[6][n, :, cut]
         total = jnp.where(alive, total, 0.0)
-        back_home = grads[RAW, :, cut]
+        back_home = kind[2][RAW, :, cut]
         for b in range(atoms):
             back_home = back_home + jnp.where(homes[b], total[b : b + 1, :], 0.0)
         return back_home
@@ -559,24 +583,17 @@
     for h in range(halves):
         cs, cv = cotans[h]
         cut = slice(h * 128, h * 128 + 128)
-        gscal_ref[:, cut] = final(h * 128) + cs
+        gscal_ref[:, cut] = final(features, h * 128) + cs
         for a in range(3):
-            gvec_ref[a, :, cut] = final((a + 1) * channels + h * 128) + cv[a]
-    pull = jnp.sum(d_apart, axis=0) - final(width)
+            gvec_ref[a, :, cut] = final(features, (a + 1) * channels + h * 128) + cv[a]
+    pull = jnp.sum(d_apart, axis=0) - final(positions, 0)
     for a in range(3):
         forces_ref[a : a + 1, :] = row_of(pull[:, a : a + 1])
 
 
 def settle(*refs):
-    count = len(refs) // 2
-    sems = refs[-1]
-    made = [
-        pltpu.make_async_copy(refs[n], refs[count + n], sems.at[n]) for n in range(count)
-    ]
-    for m in made:
-        m.start()
-    for m in made:
-        m.wait()
+    for source, target in zip(refs[:4], refs[4:]):
+        target[...] = source[...]
 
 
 def shards(sizes):
@@ -598,7 +615,7 @@
         atoms, channels = scalars.shape
         slots = neighbour_ids.shape[0]
         edges = slots * atoms
-        packed = 4 * channels + 128
+        packed = 4 * channels
         vmem = pl.BlockSpec(memory_space=pltpu.VMEM)
         hbm = pl.BlockSpec(memory_space=pl.ANY)
         f32 = jnp.float32
@@ -634,12 +651,13 @@
             scratch_shapes=landing
             + [
                 pltpu.SemaphoreType.DMA((14,)),
-                pltpu.VMEM((RAW + 1, atoms, packed), f32),
-                pltpu.VMEM((RAW + 1, atoms, packed), f32),
-                pltpu.VMEM((18, atoms, packed), f32),
-                pltpu.VMEM((3, atoms, packed), f32),
-                pltpu.VMEM((3, atoms, packed), f32),
-                pltpu.VMEM((5, atoms, packed), f32),
+            ]
+            + [
+                pltpu.VMEM((count, atoms, row), f32)
+                for row in (packed, 128)
+                for count in (RAW + 1, RAW + 1, 18, 3, 3, 5)
+            ]
+            + [
                 pltpu.VMEM((edges, 8 * (RAW + 1)), f32),
                 pltpu.VMEM((8 * (RAW + 1), edges), f32),
                 pltpu.VMEM((slots, atoms, 4 * channels), f32),
@@ -648,10 +666,10 @@
                 pltpu.VMEM((3, slots, atoms, 128), f32),
                 pltpu.VMEM((edges, 4 * channels), jnp.bfloat16),
                 pltpu.VMEM((edges, 6 * channels), jnp.bfloat16),
-                pltpu.SemaphoreType.DMA((15,)),
-                pltpu.SemaphoreType.DMA((15,)),
-                pltpu.SemaphoreType.DMA((15,)),
-                pltpu.SemaphoreType.DMA((15,)),
+                pltpu.SemaphoreType.DMA((31,)),
+                pltpu.SemaphoreType.DMA((31,)),
+                pltpu.SemaphoreType.DMA((31,)),
+                pltpu.SemaphoreType.DMA((31,)),
                 pltpu.SemaphoreType.REGULAR((2,)),
             ],
             compiler_params=pltpu.CompilerParams(
@@ -661,9 +679,8 @@
         energies, forces, grad_scalars, grad_vectors = pl.pallas_call(
             settle,
             out_shape=out_shape,
-            in_specs=[hbm] * 4,
-            out_specs=(hbm,) * 4,
-            scratch_shapes=[pltpu.SemaphoreType.DMA((4,))],
+            in_specs=[vmem] * 4,
+            out_specs=(vmem,) * 4,
             compiler_params=pltpu.CompilerParams(vmem_limit_bytes=56 * 1024 * 1024),
         )(*results)
         return energies.reshape(-1), forces.T, grad_scalars, grad_vectors.transpose(1, 0, 2)

time: 48 us -> 45.7 us (0.952); the launches traced: 47.1 us -> 45.4 us
  Pallas kernels: 45.8 us -> 44.1 us
    pallas_call x1, Pallas kernels: 43.6 us -> 42.7 us  [run(): pl.pallas_call(functools.partial(kernel, sizes), out_shape=out_shape, in_...]
    pallas_call x1, Pallas kernels: 2.2 us -> 1.39 us  [run(): pl.pallas_call(settle, out_shape=out_shape, in_specs=[vmem] * 4, out_spec...]
where the time goes in v4:
time: 45.7 us; the launch traced here: 45.4 us
  Pallas kernels  44.1 us (96%)
  between operations  1.29 us (3%)
    pallas_call x1, Pallas kernels, run(): pl.pallas_call(functools.partial(kernel, sizes), out_shape=out_shape, in_...  42.7 us
    pallas_call x1, Pallas kernels, run(): pl.pallas_call(settle, out_shape=out_shape, in_specs=[vmem] * 4, out_spec...  1.39 us

profile of v4, /device:TPU:7, one launch (start us, length us, event | category | flops | bytes accessed | tf_op | source)
XLA Modules:
  0.0 45.4 jit_solution(8284878011515324436)
XLA Ops:
  1.3 42.7 %shard_map.156 = (f32[1,8]{1,0:T(1,128)}, f32[3,8]{1,0:T(4,128)}, f32[8,256]{1,0:T(8,128)}, f32[3,8,256]{2,1,0:T(8,128)}) custom-call(s32[1]{0:T(128)S(6)} %copy.17.count_ref, f32[3,8]{1,0:T(4,128)} %bitcast.12, f32[8,256]{1,0:T(8,128)} %scalars_hbm.1, f32[3,8,256]{2,1,0:T(8,128)} %bitcast.10, s32[1,8]{1,0:T(1,128)} %bitcast.14, s32[1,8]{1,0:T(1,128)} %bitcast.15, ...), custom_call_target="tpu_custom_call" | custom-call | tf_op jit(solution)/shard_map/pallas_call | solution.py:646
  44.0 1.4 %shard_map.157 = (f32[1,8]{1,0:T(1,128)}, f32[3,8]{1,0:T(4,128)}, f32[8,256]{1,0:T(8,128)}, f32[3,8,256]{2,1,0:T(8,128)}) custom-call(f32[1,8]{1,0:T(1,128)} %get-tuple-element.12.refs_0_, f32[3,8]{1,0:T(4,128)} %get-tuple-element.13.refs_1_, f32[8,256]{1,0:T(8,128)} %get-tuple-element.14.refs_2_, f32[3,8,256]{2,1,0:T(8,128)} %get-tuple-element.15.refs_3_), custom_call_target="tpu_custom_call" | custom-call | tf_op jit(solution)/shard_map/pallas_call | solution.py:679

commit v5 on v4

--- a/solution.py
+++ b/solution.py
@@ -645,7 +645,7 @@
         )
         results = pl.pallas_call(
             functools.partial(kernel, sizes),
-            out_shape=out_shape,
+            out_shape=tuple(pltpu.VMEM(x.shape, x.dtype) for x in out_shape),
             in_specs=[pl.BlockSpec(memory_space=pltpu.SMEM)] + [hbm] * 12,
             out_specs=(vmem,) * 4,
             scratch_shapes=landing
@@ -681,7 +681,7 @@
             out_shape=out_shape,
             in_specs=[vmem] * 4,
             out_specs=(vmem,) * 4,
-            compiler_params=pltpu.CompilerParams(vmem_limit_bytes=56 * 1024 * 1024),
+            compiler_params=pltpu.CompilerParams(vmem_limit_bytes=1024 * 1024),
         )(*results)
         return energies.reshape(-1), forces.T, grad_scalars, grad_vectors.transpose(1, 0, 2)
 

time: 45.7 us -> 44.3 us (0.969)
  Pallas kernels: 44.1 us -> 42.7 us
    pallas_call x1, Pallas kernels: 1.39 us -> 0.63 us  [run(): pl.pallas_call(settle, out_shape=out_shape, in_specs=[vmem] * 4, out_spec...]
    pallas_call x1, Pallas kernels: 42.7 us -> 42.1 us  [run(): pl.pallas_call(functools.partial(kernel, sizes), out_shape=tuple((pltpu.V...]
where the time goes in v5:
time: 44.3 us; the launch traced here: 44 us
  Pallas kernels  42.7 us (96%)
  between operations  1.29 us (3%)
    pallas_call x1, Pallas kernels, run(): pl.pallas_call(functools.partial(kernel, sizes), out_shape=tuple((pltpu.V...  42.1 us

profile of v5, /device:TPU:7, one launch (start us, length us, event | category | flops | bytes accessed | tf_op | source)
XLA Modules:
  0.0 44.0 jit_solution(7885323963189776415)
XLA Ops:
  1.3 42.1 %shard_map.156 = (f32[1,8]{1,0:T(1,128)S(1)}, f32[3,8]{1,0:T(4,128)S(1)}, f32[8,256]{1,0:T(8,128)S(1)}, f32[3,8,256]{2,1,0:T(8,128)S(1)}) custom-call(s32[1]{0:T(128)S(6)} %copy.17.count_ref, f32[3,8]{1,0:T(4,128)} %bitcast.12, f32[8,256]{1,0:T(8,128)} %scalars_hbm.1, f32[3,8,256]{2,1,0:T(8,128)} %bitcast.10, s32[1,8]{1,0:T(1,128)} %bitcast.14, ...), custom_call_target="tpu_custom_call" | custom-call | tf_op jit(solution)/shard_map/pallas_call | solution.py:646
  43.4 0.6 %shard_map.157 = (f32[1,8]{1,0:T(1,128)}, f32[3,8]{1,0:T(4,128)}, f32[8,256]{1,0:T(8,128)}, f32[3,8,256]{2,1,0:T(8,128)}) custom-call(f32[1,8]{1,0:T(1,128)S(1)} %get-tuple-element.12.refs_0_, f32[3,8]{1,0:T(4,128)S(1)} %get-tuple-element.13.refs_1_, f32[8,256]{1,0:T(8,128)S(1)} %get-tuple-element.14.refs_2_, f32[3,8,256]{2,1,0:T(8,128)S(1)} %get-tuple-element.15.refs_3_), custom_call_target="tpu_custom_call" | custom-call | tf_op jit(solution)/shard_map/pallas_call | solution.py:679

commit v6 on v5

--- a/solution.py
+++ b/solution.py
@@ -115,10 +115,8 @@
     def hello(partner):
         pl.semaphore_signal(barrier, inc=1, device_id=partner, device_id_type=MESH)
 
+    near_partners = [(near, down, gz), (near, gy, gz), (near, up, gz)]
     partners = [
-        (near, down, gz),
-        (near, gy, gz),
-        (near, up, gz),
         (gx, down, gz),
         (gx, up, gz),
         (gx, gy, left),
@@ -126,6 +124,12 @@
     ]
     for partner in partners:
         hello(partner)
+
+    @pl.when(gx != nx - 2)
+    def _():
+        for partner in near_partners:
+            hello(partner)
+
     for other in (ahead, behind):
 
         @pl.when(other > gx)
@@ -186,7 +190,13 @@
 
     level, top = lax.div(gx, 2), nx // 2 - 1
     earlier = lax.div(level + top - 1, top) + lax.div(level, top)
-    pl.semaphore_wait(barrier, len(partners) + earlier + 3 * lax.div(gx, nx - 1))
+    pl.semaphore_wait(barrier, len(partners) + 3 + earlier)
+
+    @pl.when(gx == nx - 2)
+    def _():
+        for partner in near_partners:
+            pl.semaphore_signal(ready.at[2], inc=1, device_id=partner, device_id_type=MESH)
+
 
     features = (0, table, grads, from_z, from_x, from_w, from_y)
     positions = (16, place_table, place_grads, place_z, place_x, place_w, place_y)
@@ -224,13 +234,19 @@
     sends = {0: [], 16: []}
     to_near, to_side = {}, {}
     for kind in (positions, features):
+        to_side[kind[0]] = [
+            copy(kind, 0, (1, SELF, 1), (1, OWN), (gx, up, gz)),
+            copy(kind, 1, (1, SELF, 1), (1, OWN + 2), (gx, down, gz)),
+        ]
+
+    @pl.when(last)
+    def _():
+        pl.semaphore_wait(ready.at[2], 3)
+
+    for kind in (positions, features):
         to_near[kind[0]] = [
             copy(kind, 2 + n, (1, SELF, 1), (1, NEAR + n), (near, place, gz))
             for n, place in ((0, up), (1, gy), (2, down))
-        ]
-        to_side[kind[0]] = [
-            copy(kind, 0, (1, SELF, 1), (1, OWN), (gx, up, gz)),
-            copy(kind, 1, (1, SELF, 1), (1, OWN + 2), (gx, down, gz)),
         ]
 
     @pl.when(ahead < gx)
@@ -670,7 +686,7 @@
                 pltpu.SemaphoreType.DMA((31,)),
                 pltpu.SemaphoreType.DMA((31,)),
                 pltpu.SemaphoreType.DMA((31,)),
-                pltpu.SemaphoreType.REGULAR((2,)),
+                pltpu.SemaphoreType.REGULAR((3,)),
             ],
             compiler_params=pltpu.CompilerParams(
                 collective_id=0, has_side_effects=True, vmem_limit_bytes=56 * 1024 * 1024

time: 44.3 us -> 43.6 us (0.984)
  Pallas kernels: 42.7 us -> 41.9 us
    pallas_call x1, Pallas kernels: 42.1 us -> 41.2 us  [run(): pl.pallas_call(functools.partial(kernel, sizes), out_shape=tuple((pltpu.V...]
where the time goes in v6:
time: 43.6 us; the launch traced here: 43.1 us
  Pallas kernels  41.9 us (96%)
  between operations  1.29 us (3%)
    pallas_call x1, Pallas kernels, run(): pl.pallas_call(functools.partial(kernel, sizes), out_shape=tuple((pltpu.V...  41.2 us

profile of v6, /device:TPU:7, one launch (start us, length us, event | category | flops | bytes accessed | tf_op | source)
XLA Modules:
  0.0 43.1 jit_solution(710513434100672874)
XLA Ops:
  1.3 41.2 %shard_map.156 = (f32[1,8]{1,0:T(1,128)S(1)}, f32[3,8]{1,0:T(4,128)S(1)}, f32[8,256]{1,0:T(8,128)S(1)}, f32[3,8,256]{2,1,0:T(8,128)S(1)}) custom-call(s32[1]{0:T(128)S(6)} %copy.17.count_ref, f32[3,8]{1,0:T(4,128)} %bitcast.12, f32[8,256]{1,0:T(8,128)} %scalars_hbm.1, f32[3,8,256]{2,1,0:T(8,128)} %bitcast.10, s32[1,8]{1,0:T(1,128)} %bitcast.14, ...), custom_call_target="tpu_custom_call" | custom-call | tf_op jit(solution)/shard_map/pallas_call | solution.py:662
  42.5 0.6 %shard_map.157 = (f32[1,8]{1,0:T(1,128)}, f32[3,8]{1,0:T(4,128)}, f32[8,256]{1,0:T(8,128)}, f32[3,8,256]{2,1,0:T(8,128)}) custom-call(f32[1,8]{1,0:T(1,128)S(1)} %get-tuple-element.12.refs_0_, f32[3,8]{1,0:T(4,128)S(1)} %get-tuple-element.13.refs_1_, f32[8,256]{1,0:T(8,128)S(1)} %get-tuple-element.14.refs_2_, f32[3,8,256]{2,1,0:T(8,128)S(1)} %get-tuple-element.15.refs_3_), custom_call_target="tpu_custom_call" | custom-call | tf_op jit(solution)/shard_map/pallas_call | solution.py:695

commit v7 on v6

--- a/solution.py
+++ b/solution.py
@@ -109,7 +109,7 @@
     right, left = lax.rem(gz + 1, nz), lax.rem(gz + nz - 1, nz)
 
     first, last = gx == 0, gx == nx - 1
-    three = ((0, down), (1, gy), (2, up))
+    three = ((1, gy), (0, down), (2, up))
     barrier = pltpu.get_barrier_semaphore()
 
     def hello(partner):
@@ -565,7 +565,7 @@
         for n, place in ((0, down), (1, gy), (2, up)):
             pending.append(copy(kind, 2 + n, (2, NEAR + n, 1), (6, 4 - n), (near, place, gz), back))
     for made in pending:
-        made.wait()
+        made.wait_recv()
 
     @pl.when(first)
     def _():
@@ -573,16 +573,6 @@
             for made in direct_back[kind[0]]:
                 made.wait_recv()
             kind[2][SELF] += kind[5][0] + kind[5][1] + kind[5][2]
-
-    @pl.when(gx != nx - 1)
-    def _():
-        for kind in (features, positions):
-            far_copy[kind[0]].wait_send()
-
-    @pl.when(last)
-    def _():
-        for made in direct_back[0] + direct_back[16]:
-            made.wait_send()
 
     def final(kind, c):
         cut = slice(c, c + 128)
@@ -605,6 +595,19 @@
     pull = jnp.sum(d_apart, axis=0) - final(positions, 0)
     for a in range(3):
         forces_ref[a : a + 1, :] = row_of(pull[:, a : a + 1])
+
+    for made in pending:
+        made.wait_send()
+
+    @pl.when(gx != nx - 1)
+    def _():
+        for kind in (features, positions):
+            far_copy[kind[0]].wait_send()
+
+    @pl.when(last)
+    def _():
+        for made in direct_back[0] + direct_back[16]:
+            made.wait_send()
 
 
 def settle(*refs):

time: 43.6 us -> 43.6 us (level)
  no operation moved by 1% of the time
where the time goes in v7:
time: 43.6 us; the launch traced here: 43.2 us
  Pallas kernels  41.9 us (96%)
  between operations  1.29 us (3%)
    pallas_call x1, Pallas kernels, run(): pl.pallas_call(functools.partial(kernel, sizes), out_shape=tuple((pltpu.V...  41.2 us

profile of v7, /device:TPU:7, one launch (start us, length us, event | category | flops | bytes accessed | tf_op | source)
XLA Modules:
  0.0 43.2 jit_solution(17020107198694854091)
XLA Ops:
  1.3 41.2 %shard_map.156 = (f32[1,8]{1,0:T(1,128)S(1)}, f32[3,8]{1,0:T(4,128)S(1)}, f32[8,256]{1,0:T(8,128)S(1)}, f32[3,8,256]{2,1,0:T(8,128)S(1)}) custom-call(s32[1]{0:T(128)S(6)} %copy.17.count_ref, f32[3,8]{1,0:T(4,128)} %bitcast.12, f32[8,256]{1,0:T(8,128)} %scalars_hbm.1, f32[3,8,256]{2,1,0:T(8,128)} %bitcast.10, s32[1,8]{1,0:T(1,128)} %bitcast.14, ...), custom_call_target="tpu_custom_call" | custom-call | tf_op jit(solution)/shard_map/pallas_call | solution.py:665
  42.5 0.6 %shard_map.157 = (f32[1,8]{1,0:T(1,128)}, f32[3,8]{1,0:T(4,128)}, f32[8,256]{1,0:T(8,128)}, f32[3,8,256]{2,1,0:T(8,128)}) custom-call(f32[1,8]{1,0:T(1,128)S(1)} %get-tuple-element.12.refs_0_, f32[3,8]{1,0:T(4,128)S(1)} %get-tuple-element.13.refs_1_, f32[8,256]{1,0:T(8,128)S(1)} %get-tuple-element.14.refs_2_, f32[3,8,256]{2,1,0:T(8,128)S(1)} %get-tuple-element.15.refs_3_), custom_call_target="tpu_custom_call" | custom-call | tf_op jit(solution)/shard_map/pallas_call | solution.py:698

commit v8 on v7

--- a/solution.py
+++ b/solution.py
@@ -280,6 +280,13 @@
     hot_t[...] = hot_f32.T
 
     def along_z(kind, g):
+        if kind is positions:
+            if g == 2:
+                sends[kind[0]] += [
+                    copy(kind, 10, (1, OWN, 9), (1, 0), (gx, gy, right)),
+                    copy(kind, 11, (1, OWN, 9), (1, 18), (gx, gy, left)),
+                ]
+            return
         sends[kind[0]] += [
             copy(kind, 6 + 2 * g, (1, OWN + 3 * g, 3), (1, 3 * g), (gx, gy, right)),
             copy(kind, 7 + 2 * g, (1, OWN + 3 * g, 3), (1, 18 + 3 * g), (gx, gy, left)),

time: 43.6 us -> 44.2 us (1.014)
  the two profiles are of different devices: /device:TPU:7 before, /device:TPU:15 now
where the time goes in v8:
time: 44.2 us; the launch traced here: 44.1 us
  Pallas kernels  42.8 us (97%)
  between operations  1.29 us (3%)
    pallas_call x1, Pallas kernels, run(): pl.pallas_call(functools.partial(kernel, sizes), out_shape=tuple((pltpu.V...  42.2 us

profile of v8, /device:TPU:15, one launch (start us, length us, event | category | flops | bytes accessed | tf_op | source)
XLA Modules:
  0.0 44.1 jit_solution(17873837012172794826)
XLA Ops:
  1.3 42.2 %shard_map.156 = (f32[1,8]{1,0:T(1,128)S(1)}, f32[3,8]{1,0:T(4,128)S(1)}, f32[8,256]{1,0:T(8,128)S(1)}, f32[3,8,256]{2,1,0:T(8,128)S(1)}) custom-call(s32[1]{0:T(128)S(6)} %copy.17.count_ref, f32[3,8]{1,0:T(4,128)} %bitcast.12, f32[8,256]{1,0:T(8,128)} %scalars_hbm.1, f32[3,8,256]{2,1,0:T(8,128)} %bitcast.10, s32[1,8]{1,0:T(1,128)} %bitcast.14, ...), custom_call_target="tpu_custom_call" | custom-call | tf_op jit(solution)/shard_map/pallas_call | solution.py:672
  43.5 0.6 %shard_map.157 = (f32[1,8]{1,0:T(1,128)}, f32[3,8]{1,0:T(4,128)}, f32[8,256]{1,0:T(8,128)}, f32[3,8,256]{2,1,0:T(8,128)}) custom-call(f32[1,8]{1,0:T(1,128)S(1)} %get-tuple-element.12.refs_0_, f32[3,8]{1,0:T(4,128)S(1)} %get-tuple-element.13.refs_1_, f32[8,256]{1,0:T(8,128)S(1)} %get-tuple-element.14.refs_2_, f32[3,8,256]{2,1,0:T(8,128)S(1)} %get-tuple-element.15.refs_3_), custom_call_target="tpu_custom_call" | custom-call | tf_op jit(solution)/shard_map/pallas_call | solution.py:705
